TPU v7x, 128 devices: a whole 4x4x4 slice. The times are simulated.
128 devices in a mesh: pipe: 2 (over y_lo), shard: 4 (over y_hi, core), rep: 16 (over z, x).
Axes of the slice: x: 4, y: 4 (y_hi: 2, y_lo: 2; y = y_hi * 2 + y_lo), z: 4, core: 2. Of those that a mesh axis runs over, the one named last changes fastest.
Arguments:
- images: bfloat16 [256, 196, 512], P(('shard', 'rep')), may hold values from -6 to 6
- cotangent: bfloat16 [256, 196, 512], P(('shard', 'rep')), may hold values from -6 to 6
- micro_order: int32 [64, 4], P(('shard', 'rep')), may hold values from 0 to 3, each once within a row
- region_ids: int32 [196], replicated, may hold values from 0 to 3
- rel_index: int32 [49, 49], replicated, may hold values from 0 to 168
- qkv_weight: bfloat16 [2, 512, 1536], P('pipe', 'shard'), may hold values from -0.25 to 0.25
- proj_weight: bfloat16 [2, 512, 512], P('pipe', 'shard'), may hold values from -0.5 to 0.5
- up_weight: bfloat16 [2, 512, 2048], P('pipe', 'shard'), may hold values from -0.25 to 0.25
- down_weight: bfloat16 [2, 2048, 512], P('pipe', 'shard'), may hold values from -0.125 to 0.125
- bias_table: bfloat16 [2, 169, 16], P('pipe', None, 'shard'), may hold values from -4 to 4
- norm_gains: bfloat16 [2, 2, 512], P('pipe', None, 'shard'), may hold values from 0.5 to 1.5
- offsets: bfloat16 [2, 6, 512], P('pipe', None, 'shard'), may hold values from -2 to 2
- hidden_bias: bfloat16 [2, 2048], P('pipe', 'shard'), may hold values from -2 to 2
Outputs:
- layer_outputs: bfloat16 [2, 256, 196, 512], P('pipe', ('shard', 'rep'))
- input_grads: float32 [2, 256, 196, 512], P('pipe', ('shard', 'rep'))
- qkv_grad: float32 [2, 512, 1536], P('pipe', 'shard')
- proj_grad: float32 [2, 512, 512], P('pipe', 'shard')
- up_grad: float32 [2, 512, 2048], P('pipe', 'shard')
- down_grad: float32 [2, 2048, 512], P('pipe', 'shard')
- table_grad: float32 [2, 169, 16], P('pipe', None, 'shard')
- gains_grad: float32 [2, 2, 512], P('pipe', None, 'shard')
- offsets_grad: float32 [2, 6, 512], P('pipe', None, 'shard')
- hidden_grad: float32 [2, 2048], P('pipe', 'shard')
Inputs may be any that keep to these rules, and one draw needn't show every extreme that they name: `micro_order`: each row names every one of its group's 4 images once.
All inputs are finite; a program needn't handle non-finite values.
Results may differ from a plain program's by a relative error of at most 0.024.
Values may be sent and summed in bfloat16 or wider, within the bound.
A program may use at most 192 MiB of HBM per device.

v0:
```python
import jax
import jax.numpy as jnp
from jax import lax
from jax.sharding import PartitionSpec as P

SIDE = 14
WIN = 7
SHIFT = 3
MICRO = 4


exact_precision = lax.Precision.HIGHEST


def passed_along(block, axis, distance):
    devices = range(lax.axis_size(axis))
    route = [(i - distance, i) for i in devices if i - distance in devices]
    return lax.ppermute(block, axis, route)


def layer_norm(tensor, gain_scale, offset):
    average = jnp.mean(tensor, -1, keepdims=True)
    centred = tensor - average
    variance = jnp.mean(centred * centred, -1, keepdims=True)
    return centred * lax.rsqrt(variance + 1e-05) * gain_scale + offset


def exact_gelu(tensor):
    return jax.nn.gelu(tensor, approximate=False)


def roll_grid(tensor, amount):
    batch_size, model_width = (tensor.shape[0], tensor.shape[2])
    grid = tensor.reshape(batch_size, SIDE, SIDE, model_width)
    grid = jnp.roll(jnp.roll(grid, amount, 1), amount, 2)
    return grid.reshape(batch_size, SIDE * SIDE, model_width)


def to_windows(tensor):
    batch_size, model_width = (tensor.shape[0], tensor.shape[2])
    grid = tensor.reshape(batch_size, SIDE // WIN, WIN, SIDE // WIN, WIN, model_width)
    grid = grid.transpose(0, 1, 3, 2, 4, 5)
    return grid.reshape(-1, WIN * WIN, model_width)


def from_windows(window_blocks, batch_size):
    model_width = window_blocks.shape[2]
    grid = window_blocks.reshape(batch_size, SIDE // WIN, SIDE // WIN, WIN, WIN, model_width)
    grid = grid.transpose(0, 1, 3, 2, 4, 5)
    return grid.reshape(batch_size, SIDE * SIDE, model_width)


def layer_forward(inputs, weights, shift_by, one_hot, mask_add):
    (
        query_key_value_weight,
        output_projection_weight,
        w_up,
        w_down,
        table,
        gains,
        offset_rows,
        hidden_bias,
    ) = weights
    batch_size, model_width = (inputs.shape[0], inputs.shape[2])
    head_count = table.shape[1]
    head_width = model_width // head_count
    window_tokens = WIN * WIN
    gain_rows = gains.astype(jnp.float32)
    offset_numbers = offset_rows.astype(jnp.float32)
    normed = layer_norm(inputs, gain_rows[0], offset_numbers[0]).astype(jnp.bfloat16)
    window_blocks = to_windows(roll_grid(normed, -shift_by))
    bias_entries = jnp.concatenate(
        [offset_numbers[2], jnp.zeros((model_width,), jnp.float32), offset_numbers[3]]
    )
    projected_output = (
        jnp.einsum(
            "ngs,sa->nga", window_blocks, query_key_value_weight, preferred_element_type=jnp.float32
        )
        + bias_entries
    ).astype(jnp.bfloat16)
    split_heads = projected_output.reshape(-1, window_tokens, 3, head_count, head_width)
    queries, key_heads, values = (split_heads[:, :, 0], split_heads[:, :, 1], split_heads[:, :, 2])
    rel_bias = jnp.dot(one_hot, table.astype(jnp.float32), precision=exact_precision)
    rel_bias = rel_bias.reshape(window_tokens, window_tokens, head_count).transpose(2, 0, 1)
    scores = jnp.einsum(
        "bqhe,bkhe->bhqk", queries, key_heads, preferred_element_type=jnp.float32
    ) * head_width ** (-0.5)
    scores = (
        scores.reshape(batch_size, -1, head_count, window_tokens, window_tokens)
        + mask_add[None, :, None]
        + rel_bias[None, None]
    )
    scores = scores.reshape(-1, head_count, window_tokens, window_tokens)
    highest = jnp.max(scores, -1, keepdims=True)
    exponent = jnp.exp(scores - highest)
    attn_prob = exponent / jnp.sum(exponent, -1, keepdims=True)
    attended_values = jnp.einsum(
        "bhqk,bkhe->bqhe",
        attn_prob.astype(jnp.bfloat16),
        values,
        preferred_element_type=jnp.float32,
    )
    attended_values = attended_values.reshape(-1, window_tokens, model_width).astype(jnp.bfloat16)
    branch_output = (
        jnp.einsum(
            "ngs,sa->nga",
            attended_values,
            output_projection_weight,
            preferred_element_type=jnp.float32,
        )
        + offset_numbers[4]
    )
    mixed_sum = inputs + roll_grid(from_windows(branch_output, batch_size), shift_by)
    second_norm = layer_norm(mixed_sum, gain_rows[1], offset_numbers[1]).astype(jnp.bfloat16)
    hidden = jnp.einsum(
        "btd,df->btf", second_norm, w_up, preferred_element_type=jnp.float32
    ) + hidden_bias.astype(jnp.float32)
    active = exact_gelu(hidden).astype(jnp.bfloat16)
    result = (
        mixed_sum
        + jnp.einsum("btf,fd->btd", active, w_down, preferred_element_type=jnp.float32)
        + offset_numbers[5]
    )
    kept = (
        inputs,
        mixed_sum,
        window_blocks,
        projected_output,
        attn_prob,
        attended_values,
        second_norm,
        hidden,
        active,
    )
    return (result.astype(jnp.bfloat16), kept)


def layer_backward(incoming, kept, weights, shift_by, one_hot):
    (
        inputs,
        mixed_sum,
        window_blocks,
        projected_output,
        attn_prob,
        attended_values,
        second_norm,
        hidden,
        active,
    ) = kept
    (
        query_key_value_weight,
        output_projection_weight,
        w_up,
        w_down,
        table,
        gains,
        offset_rows,
        hidden_bias,
    ) = weights
    batch_size, model_width = (inputs.shape[0], inputs.shape[2])
    head_count = table.shape[1]
    head_width = model_width // head_count
    window_tokens = WIN * WIN
    gain_rows = gains.astype(jnp.float32)
    offset_numbers = offset_rows.astype(jnp.float32)
    incoming_low = incoming.astype(jnp.bfloat16)
    grad_down = jnp.einsum("btf,btd->fd", active, incoming_low, preferred_element_type=jnp.float32)
    grad_off5 = jnp.sum(incoming, (0, 1))
    d_active = jnp.einsum("btd,fd->btf", incoming_low, w_down, preferred_element_type=jnp.float32)
    _, gelu_pull = jax.vjp(exact_gelu, hidden)
    d_hidden = gelu_pull(d_active)[0].astype(jnp.bfloat16)
    grad_up = jnp.einsum("btd,btf->df", second_norm, d_hidden, preferred_element_type=jnp.float32)
    grad_hidden = jnp.sum(d_hidden.astype(jnp.float32), (0, 1))
    d_second = jnp.einsum("btf,df->btd", d_hidden, w_up, preferred_element_type=jnp.float32)
    _, norm_pull = jax.vjp(layer_norm, mixed_sum, gain_rows[1], offset_numbers[1])
    d_mixed_part, grad_gain1, grad_off1 = norm_pull(d_second)
    d_mixed = incoming + d_mixed_part
    branch_gradient = to_windows(roll_grid(d_mixed, -shift_by)).astype(jnp.bfloat16)
    projection_weight_gradient = jnp.einsum(
        "mzv,mza->va", attended_values, branch_gradient, preferred_element_type=jnp.float32
    )
    grad_off4 = jnp.sum(branch_gradient.astype(jnp.float32), (0, 1))
    d_attended = jnp.einsum(
        "tjk,fk->tjf", branch_gradient, output_projection_weight, preferred_element_type=jnp.float32
    ).astype(jnp.bfloat16)
    d_attended = d_attended.reshape(-1, window_tokens, head_count, head_width)
    split_heads = projected_output.reshape(-1, window_tokens, 3, head_count, head_width)
    queries, key_heads, values = (split_heads[:, :, 0], split_heads[:, :, 1], split_heads[:, :, 2])
    d_prob = jnp.einsum("bqhe,bkhe->bhqk", d_attended, values, preferred_element_type=jnp.float32)
    d_values = jnp.einsum(
        "bhqk,bqhe->bkhe",
        attn_prob.astype(jnp.bfloat16),
        d_attended,
        preferred_element_type=jnp.float32,
    )
    d_scores = attn_prob * (d_prob - jnp.sum(d_prob * attn_prob, -1, keepdims=True))
    d_scores = d_scores.astype(jnp.bfloat16)
    rel_sum = (
        jnp.sum(d_scores.astype(jnp.float32), 0)
        .transpose(1, 2, 0)
        .reshape(window_tokens * window_tokens, head_count)
    )
    grad_table = jnp.einsum("rn,rh->nh", one_hot, rel_sum, precision=exact_precision)
    scale_by = head_width ** (-0.5)
    d_queries = (
        jnp.einsum("bhqk,bkhe->bqhe", d_scores, key_heads, preferred_element_type=jnp.float32)
        * scale_by
    )
    d_keys = (
        jnp.einsum("bhqk,bqhe->bkhe", d_scores, queries, preferred_element_type=jnp.float32)
        * scale_by
    )
    projected_gradient = (
        jnp.stack([d_queries, d_keys, d_values], 2)
        .reshape(-1, window_tokens, 3 * model_width)
        .astype(jnp.bfloat16)
    )
    query_key_value_gradient = jnp.einsum(
        "mzv,mza->va", window_blocks, projected_gradient, preferred_element_type=jnp.float32
    )
    bias_sums = jnp.sum(projected_gradient.astype(jnp.float32), (0, 1))
    grad_off2 = bias_sums[:model_width]
    grad_off3 = bias_sums[2 * model_width :]
    window_gradient = jnp.einsum(
        "tjk,fk->tjf",
        projected_gradient,
        query_key_value_weight,
        preferred_element_type=jnp.float32,
    )
    d_normed = roll_grid(from_windows(window_gradient, batch_size), shift_by)
    _, first_pull = jax.vjp(layer_norm, inputs, gain_rows[0], offset_numbers[0])
    d_input_part, grad_gain0, grad_off0 = first_pull(d_normed)
    d_input = d_mixed + d_input_part
    grad_gains = jnp.stack([grad_gain0, grad_gain1])
    grad_offsets = jnp.stack([grad_off0, grad_off1, grad_off2, grad_off3, grad_off4, grad_off5])
    return (
        d_input,
        (
            query_key_value_gradient,
            projection_weight_gradient,
            grad_up,
            grad_down,
            grad_table,
            grad_gains,
            grad_offsets,
            grad_hidden,
        ),
    )


def add_trees(totals, addition):
    if totals is None:
        return addition
    return jax.tree.map(lambda summed, addend: summed + addend, totals, addition)


def on_device(
    images,
    cotangent,
    micro_order,
    region_ids,
    rel_index,
    qkv_weight,
    proj_weight,
    up_weight,
    down_weight,
    bias_table,
    norm_gains,
    offsets,
    hidden_bias,
):
    section = lax.axis_index("pipe")
    first_section = section == 0
    shift_by = SHIFT * section
    full_weights = (
        lax.all_gather(qkv_weight[0], "shard", axis=0, tiled=True),
        lax.all_gather(proj_weight[0], "shard", axis=0, tiled=True),
        lax.all_gather(up_weight[0], "shard", axis=0, tiled=True),
        lax.all_gather(down_weight[0], "shard", axis=0, tiled=True),
        lax.all_gather(bias_table[0], "shard", axis=1, tiled=True),
        lax.all_gather(norm_gains[0], "shard", axis=1, tiled=True),
        lax.all_gather(offsets[0], "shard", axis=1, tiled=True),
        lax.all_gather(hidden_bias[0], "shard", axis=0, tiled=True),
    )
    table_rows = bias_table.shape[1]
    one_hot = (
        rel_index.reshape(-1)[:, None] == jnp.arange(table_rows, dtype=jnp.int32)[None, :]
    ).astype(jnp.float32)
    regions = to_windows(region_ids.reshape(1, -1, 1))[:, :, 0]
    allowed = jnp.logical_or(regions[:, :, None] == regions[:, None, :], first_section)
    mask_add = jnp.where(allowed, 0.0, -1000000000.0).astype(jnp.float32)
    group_size = images.shape[0] // MICRO
    slot_order = micro_order[0]
    received = jnp.zeros((group_size,) + images.shape[1:], jnp.bfloat16)
    kept_list = []
    output_list = []
    for step_index in range(MICRO + 1):
        if step_index < MICRO:
            own_input = jnp.take(
                images, slot_order[step_index * group_size : (step_index + 1) * group_size], axis=0
            )
        else:
            own_input = jnp.zeros_like(received)
        layer_input = jnp.where(first_section, own_input, received).astype(jnp.float32)
        layer_result, kept = layer_forward(layer_input, full_weights, shift_by, one_hot, mask_add)
        kept_list.append(kept)
        output_list.append(layer_result)
        if step_index < MICRO:
            received = passed_along(layer_result, "pipe", 1)
    layer_out = jnp.where(
        first_section, jnp.concatenate(output_list[:MICRO], 0), jnp.concatenate(output_list[1:], 0)
    )
    back_weights = (
        lax.all_gather(qkv_weight[0], "shard", axis=0, tiled=True),
        lax.all_gather(proj_weight[0], "shard", axis=0, tiled=True),
        lax.all_gather(up_weight[0], "shard", axis=0, tiled=True),
        lax.all_gather(down_weight[0], "shard", axis=0, tiled=True),
        lax.all_gather(bias_table[0], "shard", axis=1, tiled=True),
        lax.all_gather(norm_gains[0], "shard", axis=1, tiled=True),
        lax.all_gather(offsets[0], "shard", axis=1, tiled=True),
        lax.all_gather(hidden_bias[0], "shard", axis=0, tiled=True),
    )
    totals = None
    grad_list = []
    received = jnp.zeros((group_size,) + images.shape[1:], jnp.bfloat16)
    for step_index in range(MICRO + 1):
        micro_index = MICRO - 1 - step_index
        if step_index < MICRO:
            target = cotangent[micro_index * group_size : (micro_index + 1) * group_size]
        else:
            target = jnp.zeros_like(received)
        arriving = jnp.where(first_section, received, target).astype(jnp.float32)
        d_input, grads = layer_backward(
            arriving, kept_list[MICRO - step_index], back_weights, shift_by, one_hot
        )
        grad_list.append(d_input)
        shares = (
            lax.psum_scatter(
                grads[0].astype(jnp.bfloat16), "shard", scatter_dimension=0, tiled=True
            ).astype(jnp.float32),
            lax.psum_scatter(
                grads[1].astype(jnp.bfloat16), "shard", scatter_dimension=0, tiled=True
            ).astype(jnp.float32),
            lax.psum_scatter(
                grads[2].astype(jnp.bfloat16), "shard", scatter_dimension=0, tiled=True
            ).astype(jnp.float32),
            lax.psum_scatter(
                grads[3].astype(jnp.bfloat16), "shard", scatter_dimension=0, tiled=True
            ).astype(jnp.float32),
            lax.psum_scatter(
                grads[4].astype(jnp.bfloat16), "shard", scatter_dimension=1, tiled=True
            ).astype(jnp.float32),
            lax.psum_scatter(
                grads[5].astype(jnp.bfloat16), "shard", scatter_dimension=1, tiled=True
            ).astype(jnp.float32),
            lax.psum_scatter(
                grads[6].astype(jnp.bfloat16), "shard", scatter_dimension=1, tiled=True
            ).astype(jnp.float32),
            lax.psum_scatter(
                grads[7].astype(jnp.bfloat16), "shard", scatter_dimension=0, tiled=True
            ).astype(jnp.float32),
        )
        summed_shares = (
            lax.psum(shares[0].astype(jnp.bfloat16), "rep").astype(jnp.float32),
            lax.psum(shares[1].astype(jnp.bfloat16), "rep").astype(jnp.float32),
            lax.psum(shares[2].astype(jnp.bfloat16), "rep").astype(jnp.float32),
            lax.psum(shares[3].astype(jnp.bfloat16), "rep").astype(jnp.float32),
            lax.psum(shares[4].astype(jnp.bfloat16), "rep").astype(jnp.float32),
            lax.psum(shares[5].astype(jnp.bfloat16), "rep").astype(jnp.float32),
            lax.psum(shares[6].astype(jnp.bfloat16), "rep").astype(jnp.float32),
            lax.psum(shares[7].astype(jnp.bfloat16), "rep").astype(jnp.float32),
        )
        totals = add_trees(totals, tuple(summed_shares))
        if step_index < MICRO:
            received = passed_along(d_input.astype(jnp.bfloat16), "pipe", -1)
    first_slots = jnp.concatenate([grad_list[MICRO - index] for index in range(MICRO)], 0)
    second_slots = jnp.concatenate([grad_list[MICRO - 1 - index] for index in range(MICRO)], 0)
    pooled = jnp.zeros_like(first_slots).at[slot_order].set(first_slots)
    input_grad = jnp.where(first_section, pooled, second_slots)
    return (
        layer_out[None],
        input_grad[None],
        totals[0][None],
        totals[1][None],
        totals[2][None],
        totals[3][None],
        totals[4][None],
        totals[5][None],
        totals[6][None],
        totals[7][None],
    )


def solution(mesh):
    return jax.shard_map(
        on_device,
        mesh=mesh,
        in_specs=(
            P(("shard", "rep"), None, None),
            P(("shard", "rep"), None, None),
            P(("shard", "rep"), None),
            P(),
            P(),
            P("pipe", "shard", None),
            P("pipe", "shard", None),
            P("pipe", "shard", None),
            P("pipe", "shard", None),
            P("pipe", None, "shard"),
            P("pipe", None, "shard"),
            P("pipe", None, "shard"),
            P("pipe", "shard"),
        ),
        out_specs=(
            P("pipe", ("shard", "rep"), None, None),
            P("pipe", ("shard", "rep"), None, None),
            P("pipe", "shard", None),
            P("pipe", "shard", None),
            P("pipe", "shard", None),
            P("pipe", "shard", None),
            P("pipe", None, "shard"),
            P("pipe", None, "shard"),
            P("pipe", None, "shard"),
            P("pipe", "shard"),
        ),
        check_vma=False,
    )
```

profile of v0, /device:TPU:0, one launch (start us, length us, event | category | flops | bytes accessed | tf_op | source)
XLA Modules:
  0.0 1591.2 jit_solution(7637359406377842640)
XLA Ops:
  22.2 6.5 all-gather
  28.8 6.7 all-gather.1
  38.0 6.7 all-gather.3
  46.5 11.7 all-gather.4
  58.3 7.1 all-gather.6
  86.4 7.2 multiply_convert_fusion.9
  213.4 5.7 multiply_convert_fusion.6
  627.4 37.3 %reduce-scatter.55.cloned.1.call-done = bf16[128,1536]{1,0:T(8,128)(2,1)} async-done(((bf16[512,1536]{1,0:T(8,128)(2,1)}), bf16[128,1536]{1,0:T(8,128)(2,1)}) %reduce-scatter.55.cloned.1.call-update) | async-done | bytes 393232 | tf_op jit(solution)/shard_map/reduce_scatter | solution.py:338
  664.7 37.0 %reduce-scatter.57.cloned.1.call-done = bf16[128,1536]{1,0:T(8,128)(2,1)} async-done(((bf16[512,1536]{1,0:T(8,128)(2,1)}), bf16[128,1536]{1,0:T(8,128)(2,1)}) %reduce-scatter.57.cloned.1.call-update) | async-done | bytes 393232 | tf_op jit(solution)/shard_map/reduce_scatter | solution.py:338
  701.7 37.9 %reduce-scatter.59.cloned.1.call-done = bf16[128,1536]{1,0:T(8,128)(2,1)} async-done(((bf16[512,1536]{1,0:T(8,128)(2,1)}), bf16[128,1536]{1,0:T(8,128)(2,1)}) %reduce-scatter.59.cloned.1.call-update) | async-done | bytes 393232 | tf_op jit(solution)/shard_map/reduce_scatter | solution.py:338
  739.6 40.2 %reduce-scatter.71.cloned.1.call-done = bf16[128,2048]{1,0:T(8,128)(2,1)} async-done(((bf16[512,2048]{1,0:T(8,128)(2,1)}), bf16[128,2048]{1,0:T(8,128)(2,1)}) %reduce-scatter.71.cloned.1.call-update) | async-done | bytes 524304 | tf_op jit(solution)/shard_map/reduce_scatter | solution.py:344
  779.9 40.4 %reduce-scatter.81.cloned.1.call-done = bf16[512,512]{1,0:T(8,128)(2,1)} async-done(((bf16[2048,512]{1,0:T(8,128)(2,1)}), bf16[512,512]{1,0:T(8,128)(2,1)}) %reduce-scatter.81.cloned.1.call-update) | async-done | bytes 524304 | tf_op jit(solution)/shard_map/reduce_scatter | solution.py:347
  820.3 40.3 %reduce-scatter.73.cloned.1.call-done = bf16[128,2048]{1,0:T(8,128)(2,1)} async-done(((bf16[512,2048]{1,0:T(8,128)(2,1)}), bf16[128,2048]{1,0:T(8,128)(2,1)}) %reduce-scatter.73.cloned.1.call-update) | async-done | bytes 524304 | tf_op jit(solution)/shard_map/reduce_scatter | solution.py:344
  860.6 40.4 %reduce-scatter.83.cloned.1.call-done = bf16[512,512]{1,0:T(8,128)(2,1)} async-done(((bf16[2048,512]{1,0:T(8,128)(2,1)}), bf16[512,512]{1,0:T(8,128)(2,1)}) %reduce-scatter.83.cloned.1.call-update) | async-done | bytes 524304 | tf_op jit(solution)/shard_map/reduce_scatter | solution.py:347
  901.0 40.3 %reduce-scatter.75.cloned.1.call-done = bf16[128,2048]{1,0:T(8,128)(2,1)} async-done(((bf16[512,2048]{1,0:T(8,128)(2,1)}), bf16[128,2048]{1,0:T(8,128)(2,1)}) %reduce-scatter.75.cloned.1.call-update) | async-done | bytes 524304 | tf_op jit(solution)/shard_map/reduce_scatter | solution.py:344
  941.3 40.6 %reduce-scatter.85.cloned.1.call-done = bf16[512,512]{1,0:T(8,128)(2,1)} async-done(((bf16[2048,512]{1,0:T(8,128)(2,1)}), bf16[512,512]{1,0:T(8,128)(2,1)}) %reduce-scatter.85.cloned.1.call-update) | async-done | bytes 524304 | tf_op jit(solution)/shard_map/reduce_scatter | solution.py:347
  981.9 40.3 %reduce-scatter.77.cloned.1.call-done = bf16[128,2048]{1,0:T(8,128)(2,1)} async-done(((bf16[512,2048]{1,0:T(8,128)(2,1)}), bf16[128,2048]{1,0:T(8,128)(2,1)}) %reduce-scatter.77.cloned.1.call-update) | async-done | bytes 524304 | tf_op jit(solution)/shard_map/reduce_scatter | solution.py:344
  1022.2 40.6 %reduce-scatter.87.cloned.1.call-done = bf16[512,512]{1,0:T(8,128)(2,1)} async-done(((bf16[2048,512]{1,0:T(8,128)(2,1)}), bf16[512,512]{1,0:T(8,128)(2,1)}) %reduce-scatter.87.cloned.1.call-update) | async-done | bytes 524304 | tf_op jit(solution)/shard_map/reduce_scatter | solution.py:347
  1062.8 40.4 %reduce-scatter.79.cloned.1.call-done = bf16[128,2048]{1,0:T(8,128)(2,1)} async-done(((bf16[512,2048]{1,0:T(8,128)(2,1)}), bf16[128,2048]{1,0:T(8,128)(2,1)}) %reduce-scatter.79.cloned.1.call-update) | async-done | bytes 524304 | tf_op jit(solution)/shard_map/reduce_scatter | solution.py:344
  1103.2 40.6 %reduce-scatter.89.cloned.1.call-done = bf16[512,512]{1,0:T(8,128)(2,1)} async-done(((bf16[2048,512]{1,0:T(8,128)(2,1)}), bf16[512,512]{1,0:T(8,128)(2,1)}) %reduce-scatter.89.cloned.1.call-update) | async-done | bytes 524304 | tf_op jit(solution)/shard_map/reduce_scatter | solution.py:347
  1152.1 20.0 %reduce-scatter.91.cloned.1.call-done = bf16[128,2]{1,0:T(8,128)(2,1)} async-done(((bf16[512,2]{1,0:T(8,128)(2,1)}), bf16[128,2]{1,0:T(8,128)(2,1)}) %reduce-scatter.91.cloned.1.call-update) | async-done | bytes 528
  1172.9 27.8 %reduce-scatter.101.cloned.1.call-done = bf16[128,6]{1,0:T(8,128)(2,1)} async-done(((bf16[512,6]{1,0:T(8,128)(2,1)}), bf16[128,6]{1,0:T(8,128)(2,1)}) %reduce-scatter.101.cloned.1.call-update) | async-done | bytes 1552
  1202.9 26.1 %reduce-scatter.93.cloned.1.call-done = bf16[128,2]{1,0:T(8,128)(2,1)} async-done(((bf16[512,2]{1,0:T(8,128)(2,1)}), bf16[128,2]{1,0:T(8,128)(2,1)}) %reduce-scatter.93.cloned.1.call-update) | async-done | bytes 528
  1229.8 27.6 %reduce-scatter.103.cloned.1.call-done = bf16[128,6]{1,0:T(8,128)(2,1)} async-done(((bf16[512,6]{1,0:T(8,128)(2,1)}), bf16[128,6]{1,0:T(8,128)(2,1)}) %reduce-scatter.103.cloned.1.call-update) | async-done | bytes 1552
  1259.7 26.2 %reduce-scatter.95.cloned.1.call-done = bf16[128,2]{1,0:T(8,128)(2,1)} async-done(((bf16[512,2]{1,0:T(8,128)(2,1)}), bf16[128,2]{1,0:T(8,128)(2,1)}) %reduce-scatter.95.cloned.1.call-update) | async-done | bytes 528
  1286.8 27.8 %reduce-scatter.105.cloned.1.call-done = bf16[128,6]{1,0:T(8,128)(2,1)} async-done(((bf16[512,6]{1,0:T(8,128)(2,1)}), bf16[128,6]{1,0:T(8,128)(2,1)}) %reduce-scatter.105.cloned.1.call-update) | async-done | bytes 1552
  1316.8 26.6 %reduce-scatter.97.cloned.1.call-done = bf16[128,2]{1,0:T(8,128)(2,1)} async-done(((bf16[512,2]{1,0:T(8,128)(2,1)}), bf16[128,2]{1,0:T(8,128)(2,1)}) %reduce-scatter.97.cloned.1.call-update) | async-done | bytes 528
  1344.3 27.8 %reduce-scatter.107.cloned.1.call-done = bf16[128,6]{1,0:T(8,128)(2,1)} async-done(((bf16[512,6]{1,0:T(8,128)(2,1)}), bf16[128,6]{1,0:T(8,128)(2,1)}) %reduce-scatter.107.cloned.1.call-update) | async-done | bytes 1552
  1374.3 13.8 all-reduce.12
  1401.9 28.2 %reduce-scatter.109.cloned.1.call-done = bf16[128,6]{1,0:T(8,128)(2,1)} async-done(((bf16[512,6]{1,0:T(8,128)(2,1)}), bf16[128,6]{1,0:T(8,128)(2,1)}) %reduce-scatter.109.cloned.1.call-update) | async-done | bytes 1552
  1431.0 76.6 %all-reduce.10 = (bf16[169,4]{0,1:T(4,128)(2,1)S(1)}, bf16[169,4]{0,1:T(4,128)(2,1)S(1)}, bf16[169,4]{0,1:T(4,128)(2,1)S(1)}, bf16[169,4]{0,1:T(4,128)(2,1)S(1)}...) all-reduce(bf16[169,4]{0,1:T(4,128)(2,1)S(1)} %get-tuple-element.31, ...), channel_id=1, replica_groups=mesh['pipe'=2,'shard'=4,'rep'=16] {'rep'}, use_global_device_ids=true, to_apply=%region_110.116 | all-reduce | flops 11060 | bytes 44240 | tf_op jit(solution)/shard_map/psum | solution.py:368
  1509.9 67.6 %all-reduce.15.cloned.1.call-done = (bf16[128,1536]{1,0:T(8,128)(2,1)}, bf16[128,1536]{1,0:T(8,128)(2,1)}, bf16[128,1536]{1,0:T(8,128)(2,1)}, bf16[128,1536]{1,0...) async-done(((bf16[128,1536]{1,0:T(8,128)(2,1)}, ...) | async-done | bytes 7864336 | tf_op jit(solution)/shard_map/psum | solution.py:364
  (1147 shorter events, 599.1 us)
Async XLA Ops:
  8.7 85.6 %all-gather.16.cloned.1.call-start = ((), (), s32[]{:S(2)}) async-start(), calls=%async_computation.52 | async-start | bytes 2621440 | tf_op jit(solution)/shard_map/all_gather | solution.py:279
  9.4 615.2 %reduce-scatter.61.cloned.1.call-start = ((), (), s32[]{:S(2)}) async-start(), calls=%async_computation.35 | async-start | bytes 655360 | tf_op jit(solution)/shard_map/reduce_scatter | solution.py:341
  317.0 307.6 %reduce-scatter.63.cloned.1.call-start = ((), (), s32[]{:S(2)}) async-start(), calls=%async_computation.36 | async-start | bytes 655360 | tf_op jit(solution)/shard_map/reduce_scatter | solution.py:341
  375.1 249.5 %reduce-scatter.65.cloned.1.call-start = ((), (), s32[]{:S(2)}) async-start(), calls=%async_computation.37 | async-start | bytes 655360 | tf_op jit(solution)/shard_map/reduce_scatter | solution.py:341
  434.1 190.6 %reduce-scatter.67.cloned.1.call-start = ((), (), s32[]{:S(2)}) async-start(), calls=%async_computation.38 | async-start | bytes 655360 | tf_op jit(solution)/shard_map/reduce_scatter | solution.py:341
  489.6 135.1 %reduce-scatter.69.cloned.1.call-start = ((), (), s32[]{:S(2)}) async-start(), calls=%async_computation.39 | async-start | bytes 655360 | tf_op jit(solution)/shard_map/reduce_scatter | solution.py:341
  512.9 111.8 %reduce-scatter.51.cloned.1.call-start = ((), (), s32[]{:S(2)}) async-start(), calls=%async_computation.30 | async-start | bytes 1966080 | tf_op jit(solution)/shard_map/reduce_scatter | solution.py:338
  519.2 108.2 %reduce-scatter.53.cloned.1.call-start = ((), (), s32[]{:S(2)}) async-start(), calls=%async_computation.31 | async-start | bytes 1966080 | tf_op jit(solution)/shard_map/reduce_scatter | solution.py:338
  526.0 138.7 %reduce-scatter.55.cloned.1.call-start = ((), (), s32[]{:S(2)}) async-start(), calls=%async_computation.32 | async-start | bytes 1966080 | tf_op jit(solution)/shard_map/reduce_scatter | solution.py:338
  532.3 169.5 %reduce-scatter.57.cloned.1.call-start = ((), (), s32[]{:S(2)}) async-start(), calls=%async_computation.33 | async-start | bytes 1966080 | tf_op jit(solution)/shard_map/reduce_scatter | solution.py:338
  538.4 201.2 %reduce-scatter.59.cloned.1.call-start = ((), (), s32[]{:S(2)}) async-start(), calls=%async_computation.34 | async-start | bytes 1966080 | tf_op jit(solution)/shard_map/reduce_scatter | solution.py:338
  556.5 223.3 %reduce-scatter.71.cloned.1.call-start = ((), (), s32[]{:S(2)}) async-start(), calls=%async_computation.40 | async-start | bytes 2621440 | tf_op jit(solution)/shard_map/reduce_scatter | solution.py:344
  560.0 260.4 %reduce-scatter.81.cloned.1.call-start = ((), (), s32[]{:S(2)}) async-start(), calls=%async_computation.45 | async-start | bytes 2621440 | tf_op jit(solution)/shard_map/reduce_scatter | solution.py:347
  564.2 296.4 %reduce-scatter.73.cloned.1.call-start = ((), (), s32[]{:S(2)}) async-start(), calls=%async_computation.41 | async-start | bytes 2621440 | tf_op jit(solution)/shard_map/reduce_scatter | solution.py:344
  568.7 332.4 %reduce-scatter.83.cloned.1.call-start = ((), (), s32[]{:S(2)}) async-start(), calls=%async_computation.46 | async-start | bytes 2621440 | tf_op jit(solution)/shard_map/reduce_scatter | solution.py:347
  572.9 368.4 %reduce-scatter.75.cloned.1.call-start = ((), (), s32[]{:S(2)}) async-start(), calls=%async_computation.42 | async-start | bytes 2621440 | tf_op jit(solution)/shard_map/reduce_scatter | solution.py:344
  577.3 404.6 %reduce-scatter.85.cloned.1.call-start = ((), (), s32[]{:S(2)}) async-start(), calls=%async_computation.47 | async-start | bytes 2621440 | tf_op jit(solution)/shard_map/reduce_scatter | solution.py:347
  580.6 441.5 %reduce-scatter.77.cloned.1.call-start = ((), (), s32[]{:S(2)}) async-start(), calls=%async_computation.43 | async-start | bytes 2621440 | tf_op jit(solution)/shard_map/reduce_scatter | solution.py:344
  585.0 477.8 %reduce-scatter.87.cloned.1.call-start = ((), (), s32[]{:S(2)}) async-start(), calls=%async_computation.48 | async-start | bytes 2621440 | tf_op jit(solution)/shard_map/reduce_scatter | solution.py:347
  589.1 514.0 %reduce-scatter.79.cloned.1.call-start = ((), (), s32[]{:S(2)}) async-start(), calls=%async_computation.44 | async-start | bytes 2621440 | tf_op jit(solution)/shard_map/reduce_scatter | solution.py:344
  593.5 550.3 %reduce-scatter.89.cloned.1.call-start = ((), (), s32[]{:S(2)}) async-start(), calls=%async_computation.49 | async-start | bytes 2621440 | tf_op jit(solution)/shard_map/reduce_scatter | solution.py:347
  597.9 574.3 %reduce-scatter.91.cloned.1.call-start = ((), (), s32[]{:S(2)}) async-start(), calls=%async_computation.53 | async-start | bytes 163840
  599.2 601.5 %reduce-scatter.101.cloned.1.call-start = ((), (), s32[]{:S(2)}) async-start(), calls=%async_computation.58 | async-start | bytes 163840
  600.4 628.6 %reduce-scatter.93.cloned.1.call-start = ((), (), s32[]{:S(2)}) async-start(), calls=%async_computation.54 | async-start | bytes 163840
  602.0 655.4 %reduce-scatter.103.cloned.1.call-start = ((), (), s32[]{:S(2)}) async-start(), calls=%async_computation.59 | async-start | bytes 163840
  604.3 681.7 %reduce-scatter.95.cloned.1.call-start = ((), (), s32[]{:S(2)}) async-start(), calls=%async_computation.55 | async-start | bytes 163840
  606.5 708.1 %reduce-scatter.105.cloned.1.call-start = ((), (), s32[]{:S(2)}) async-start(), calls=%async_computation.60 | async-start | bytes 163840
  607.7 735.7 %reduce-scatter.97.cloned.1.call-start = ((), (), s32[]{:S(2)}) async-start(), calls=%async_computation.56 | async-start | bytes 163840
  609.9 762.2 %reduce-scatter.107.cloned.1.call-start = ((), (), s32[]{:S(2)}) async-start(), calls=%async_computation.61 | async-start | bytes 163840
  613.4 787.7 %reduce-scatter.99.cloned.1.call-start = ((), (), s32[]{:S(2)}) async-start(), calls=%async_computation.57 | async-start | bytes 163840
  623.0 807.1 %reduce-scatter.109.cloned.1.call-start = ((), (), s32[]{:S(2)}) async-start(), calls=%async_computation.62 | async-start | bytes 163840
  624.3 953.2 %all-reduce.15.cloned.1.call-start = ((), (), s32[]{:S(2)}) async-start(), calls=%async_computation.63 | async-start | bytes 15728640 | tf_op jit(solution)/shard_map/psum | solution.py:364
  (298 other events, 2308.0 us)
Sparse Core Ops, SparseCore 0:
  9.7 26.1 all-gather.11
  37.6 28.8 all-gather.13
  68.2 25.9 all-gather.15
  317.1 32.6 reduce-scatter.60
  375.3 31.9 reduce-scatter.62
  434.2 31.9 reduce-scatter.64
  489.7 31.9 reduce-scatter.66
  525.0 27.9 reduce-scatter.68
  555.8 34.4 reduce-scatter.50
  592.8 34.4 reduce-scatter.52
  630.2 34.4 reduce-scatter.54
  667.2 34.4 reduce-scatter.56
  705.1 34.4 reduce-scatter.58
  742.1 37.7 reduce-scatter.70
  782.5 37.7 reduce-scatter.80
  822.8 37.7 reduce-scatter.72
  863.3 37.7 reduce-scatter.82
  903.5 37.7 reduce-scatter.74
  944.1 37.7 reduce-scatter.84
  984.4 37.7 reduce-scatter.76
  1025.0 37.7 reduce-scatter.86
  1065.4 37.7 reduce-scatter.78
  1106.0 37.7 reduce-scatter.88
  1146.2 25.9 reduce-scatter.90
  1203.1 25.8 reduce-scatter.92
  1231.6 25.8 reduce-scatter.102
  1260.0 25.8 reduce-scatter.94
  1288.6 25.8 reduce-scatter.104
  1317.5 25.8 reduce-scatter.96
  1375.2 25.8 reduce-scatter.98
  1404.2 25.8 reduce-scatter.108
  1436.2 141.2 all-reduce.14
  (2 shorter events, 51.6 us)
where the time goes:
time: 1600 us; the launch traced here: 1590 us
  waiting for transfers between devices  866 us (54%)
  local copies, waits for them, and re-layouts  240 us (15%)
  matrix products  204 us (13%)
  blocking collectives  129 us (8%)
  other arithmetic  101 us (6%)
  between operations  27.9 us (2%)
  starting transfers between devices  23.9 us (1%)
    unnamed x44, waiting for transfers between devices  246 us
    reduce_scatter x5, waiting for transfers between devices, on_device(): lax.psum_scatter(grads[3].astype(jnp.bfloat16), 'shard', scatter_dimensio...  203 us
    reduce_scatter x5, waiting for transfers between devices, on_device(): lax.psum_scatter(grads[2].astype(jnp.bfloat16), 'shard', scatter_dimensio...  201 us
    reduce_scatter x5, waiting for transfers between devices, on_device(): lax.psum_scatter(grads[0].astype(jnp.bfloat16), 'shard', scatter_dimensio...  115 us
    unnamed x624, local copies, waits for them, and re-layouts  76.8 us
    psum x1, blocking collectives, on_device(): lax.psum(shares[4].astype(jnp.bfloat16), 'rep').astype(jnp.float32)  76.6 us
    psum x1, waiting for transfers between devices, on_device(): lax.psum(shares[0].astype(jnp.bfloat16), 'rep').astype(jnp.float32)  67.6 us
    convert_element_type x15, local copies, waits for them, and re-layouts, layer_backward(): projected_gradient = jnp.stack([d_queries, d_keys, d_values], 2).reshape(...  60 us
  transfers between devices with their start and end apart: 42, of which 34 were waited for; matrix products, arithmetic and copies ran while one was open for 21% of the time, Pallas kernels for 0%

commit v1 on v0

v1 whole, which is shorter than its diff:
```python
import functools
import math

import jax
import jax.numpy as jnp
import numpy as np
from jax import lax
from jax.experimental import pallas as pl
from jax.experimental.pallas import tpu as pltpu
from jax.sharding import PartitionSpec as P

SIDE = 14
WIN = 7
SHIFT = 3
D = 512
FF = 2048
HEAD = 32
TOK = SIDE * SIDE
WTOK = WIN * WIN
WPAD = 56
PAIR = 2 * WPAD
IMG_ROWS = 4 * WPAD
IMGS = 2
ROWS = IMGS * IMG_ROWS
PAIRS = ROWS // PAIR
KEYS = 128
KROWS = ROWS + KEYS - PAIR
OUT_ROWS = 208
RELS_PAD = 256
QKV0, PROJ0, UP0, DOWN0, PACKED = 0, 1536, 2048, 4096, 6144
CHUNK = 256
SCALE = HEAD ** (-0.5)
BLOCKED = -1e30
VMEM_LIMIT = 60 * 1024 * 1024
BF16 = jnp.bfloat16
F32 = jnp.float32


def window_places(shift):
    place = np.zeros((TOK,), np.int64)
    for wr in range(2):
        for wc in range(2):
            for i in range(WIN):
                for j in range(WIN):
                    a = (wr * WIN + i + shift) % SIDE
                    b = (wc * WIN + j + shift) % SIDE
                    place[a * SIDE + b] = (wr * 2 + wc) * WPAD + i * WIN + j
    return place


def order_matrix(shift):
    matrix = np.zeros((IMG_ROWS, TOK), np.float32)
    matrix[window_places(shift), np.arange(TOK)] = 1.0
    return matrix


def back_matrix(shift):
    matrix = np.zeros((OUT_ROWS, IMG_ROWS), np.float32)
    matrix[:TOK] = order_matrix(shift).T
    return matrix


def turn_matrix(from_shift, to_shift):
    return order_matrix(to_shift) @ order_matrix(from_shift).T


def dot(a, b, dims=((1,), (0,))):
    return lax.dot_general(a, b, (dims, ((), ())), preferred_element_type=F32)


def normalised(x):
    mean = jnp.mean(x, -1, keepdims=True)
    centred = x - mean
    rstd = lax.rsqrt(jnp.mean(centred * centred, -1, keepdims=True) + 1e-5)
    return centred * rstd, rstd


def head_masks(rows):
    lane = lax.broadcasted_iota(jnp.int32, (rows, 128), 1) // HEAD
    return [lane == h for h in range(4)]


def spread_heads(block, masks):
    zero = jnp.zeros_like(block)
    return jnp.concatenate([jnp.where(m, block, zero) for m in masks], axis=0)


def join_heads(stacked, masks):
    total = None
    for h, m in enumerate(masks):
        part = jnp.where(m, stacked[h * PAIR : (h + 1) * PAIR], 0.0)
        total = part if total is None else total + part
    return total


def probabilities(q4, k, rel_ref, mask_ref, i, g):
    s = dot(q4, k, ((1,), (1,))) * SCALE
    bias = rel_ref[pl.ds(g * 4, 4)].astype(F32) + mask_ref[lax.rem(i, 2)][None]
    s = s + bias.reshape(4 * PAIR, KEYS)
    e = jnp.exp(s - jnp.max(s, -1, keepdims=True))
    return e / jnp.sum(e, -1, keepdims=True)


def down_chunk(w_ref, c):
    row = pl.multiple_of((c // 2) * 128, 128)
    col = pl.multiple_of(DOWN0 + (c % 2) * 1024, 128)
    first = w_ref[pl.ds(row, 128), pl.ds(col, D)]
    second = w_ref[pl.ds(row, 128), pl.ds(col + D, D)]
    return jnp.concatenate([first, second], axis=0)


def forward_kernel(
    turned, x_ref, w_ref, small_ref, qbias_ref, hbias_ref, rel_ref, mask_ref, back_ref, turn_ref,
    qkv_ref, o_ref, r_ref, act_ref, slope_ref, out_ref, *rest
):
    if turned:
        next_ref, low_ref, acc_ref = rest
    else:
        low_ref, acc_ref = rest
    x = x_ref[...].astype(F32)
    n1, _ = normalised(x)
    low_ref[...] = (n1 * small_ref[0:1] + small_ref[2:3]).astype(BF16)
    qkv_ref[ROWS:, :] = jnp.zeros((KROWS - ROWS, 3 * D), BF16)

    def qkv_step(n, _):
        cols = pl.ds(pl.multiple_of(n * CHUNK, CHUNK), CHUNK)
        part = dot(low_ref[...], w_ref[:, cols]) + qbias_ref[:, cols]
        qkv_ref[0:ROWS, cols] = part.astype(BF16)
        return 0

    lax.fori_loop(0, 3 * D // CHUNK, qkv_step, 0)
    masks = head_masks(PAIR)

    def attend(i, _):
        rows = pl.ds(pl.multiple_of(i * PAIR, 16), PAIR)
        keys = pl.ds(pl.multiple_of(i * PAIR, 16), KEYS)
        for g in range(4):
            q = qkv_ref[rows, g * 128 : (g + 1) * 128]
            k = qkv_ref[keys, D + g * 128 : D + (g + 1) * 128]
            v = qkv_ref[keys, 2 * D + g * 128 : 2 * D + (g + 1) * 128]
            p = probabilities(spread_heads(q, masks), k, rel_ref, mask_ref, i, g)
            o4 = dot(p.astype(BF16), v)
            o_ref[rows, g * 128 : (g + 1) * 128] = join_heads(o4, masks).astype(BF16)
        return 0

    lax.fori_loop(0, PAIRS, attend, 0)
    for n in range(D // CHUNK):
        cols = slice(n * CHUNK, (n + 1) * CHUNK)
        part = dot(o_ref[...], w_ref[:, PROJ0 + n * CHUNK : PROJ0 + (n + 1) * CHUNK])
        r_ref[:, cols] = x_ref[:, cols].astype(F32) + part + small_ref[6:7, cols]
    r = r_ref[...]
    n2, _ = normalised(r)
    low_ref[...] = (n2 * small_ref[1:2] + small_ref[3:4]).astype(BF16)
    acc_ref[...] = r + small_ref[7:8]

    def mlp(c, _):
        cols = pl.ds(pl.multiple_of(c * CHUNK, CHUNK), CHUNK)
        up = w_ref[:, pl.ds(pl.multiple_of(UP0 + c * CHUNK, CHUNK), CHUNK)]
        hid = dot(low_ref[...], up) + hbias_ref[:, cols]
        cdf = 0.5 * (1.0 + lax.erf(hid * math.sqrt(0.5)))
        act = (hid * cdf).astype(BF16)
        act_ref[:, cols] = act
        density = jnp.exp(-0.5 * hid * hid) * (1.0 / math.sqrt(2.0 * math.pi))
        slope_ref[:, cols] = (cdf + hid * density).astype(BF16)
        acc_ref[...] += dot(act, down_chunk(w_ref, c))
        return 0

    lax.fori_loop(0, FF // CHUNK, mlp, 0)
    y = acc_ref[...].astype(BF16)
    for b in range(IMGS):
        own = y[b * IMG_ROWS : (b + 1) * IMG_ROWS]
        out_ref[b] = dot(back_ref[...], own).astype(BF16)
        if turned:
            next_ref[b * IMG_ROWS : (b + 1) * IMG_ROWS] = dot(turn_ref[...], own).astype(BF16)


def backward_kernel(
    turned, dy_ref, x_ref, qkv_ref, o_ref, r_ref, act_ref, slope_ref, w_ref, small_ref, rel_ref,
    mask_ref, back_ref, turn_ref, g_ref, gsmall_ref, ghidden_ref, gbias_ref, out_ref, *rest
):
    if turned:
        next_ref, low_ref, turned_ref, dhid_ref, du_ref, dqkv_ref, do_ref = rest
    else:
        low_ref, turned_ref, dhid_ref, du_ref, dqkv_ref, do_ref = rest
    n2, rstd2 = normalised(r_ref[...])
    turned_ref[...] = (n2 * small_ref[1:2] + small_ref[3:4]).T.astype(BF16)
    du_ref[...] = jnp.zeros_like(du_ref)

    def mlp(c, _):
        cols = pl.ds(pl.multiple_of(c * CHUNK, CHUNK), CHUNK)
        up_cols = pl.ds(pl.multiple_of(UP0 + c * CHUNK, CHUNK), CHUNK)
        dy = dy_ref[...]
        dact = dot(dy, down_chunk(w_ref, c), ((1,), (1,)))
        dhid = (dact * slope_ref[:, cols].astype(F32)).astype(BF16)
        ghidden_ref[:, cols] = jnp.sum(dhid.astype(F32), 0, keepdims=True)
        down = dot(act_ref[:, cols], dy, ((0,), (0,))).astype(BF16)
        row = pl.multiple_of((c // 2) * 128, 128)
        col = pl.multiple_of(DOWN0 + (c % 2) * 1024, 128)
        g_ref[pl.ds(row, 128), pl.ds(col, D)] = down[:128]
        g_ref[pl.ds(row, 128), pl.ds(col + D, D)] = down[128:]
        g_ref[:, up_cols] = dot(turned_ref[...], dhid).astype(BF16)
        du_ref[...] += dot(dhid, w_ref[:, up_cols], ((1,), (1,)))
        return 0

    lax.fori_loop(0, FF // CHUNK, mlp, 0)
    dy = dy_ref[...].astype(F32)
    du2 = du_ref[...]
    n2, rstd2 = normalised(r_ref[...])
    z = du2 * small_ref[1:2]
    zm = jnp.mean(z, -1, keepdims=True)
    zn = jnp.mean(z * n2, -1, keepdims=True)
    dr = dy + rstd2 * (z - zm - n2 * zn)
    db = dr.astype(BF16)
    low_ref[...] = db
    gsmall_ref[1:2] = jnp.sum(du2 * n2, 0, keepdims=True)
    gsmall_ref[3:4] = jnp.sum(du2, 0, keepdims=True)
    gsmall_ref[6:7] = jnp.sum(db.astype(F32), 0, keepdims=True)
    gsmall_ref[7:8] = jnp.sum(dy, 0, keepdims=True)
    du_ref[...] = dr
    turned_ref[...] = o_ref[...].astype(F32).T.astype(BF16)
    for n in range(D // CHUNK):
        cols = slice(n * CHUNK, (n + 1) * CHUNK)
        g_ref[:, PROJ0 + n * CHUNK : PROJ0 + (n + 1) * CHUNK] = dot(
            turned_ref[...], low_ref[:, cols]
        ).astype(BF16)
        rows_of = w_ref[n * CHUNK : (n + 1) * CHUNK, PROJ0 : PROJ0 + D]
        do_ref[:, cols] = dot(low_ref[...], rows_of, ((1,), (1,))).astype(BF16)
    gbias_ref[...] = jnp.zeros_like(gbias_ref)
    masks = head_masks(PAIR)

    def attend(i, _):
        rows = pl.ds(pl.multiple_of(i * PAIR, 16), PAIR)
        keys = pl.ds(pl.multiple_of(i * PAIR, 16), KEYS)
        for g in range(4):
            here = slice(g * 128, (g + 1) * 128)
            k = qkv_ref[keys, D + g * 128 : D + (g + 1) * 128]
            v = qkv_ref[keys, 2 * D + g * 128 : 2 * D + (g + 1) * 128]
            q4 = spread_heads(qkv_ref[rows, here], masks)
            do4 = spread_heads(do_ref[rows, here], masks)
            p = probabilities(q4, k, rel_ref, mask_ref, i, g)
            dp = dot(do4, v, ((1,), (1,)))
            ds = (p * (dp - jnp.sum(dp * p, -1, keepdims=True))).astype(BF16)
            gbias_ref[g * 4 : (g + 1) * 4] += ds.astype(F32).reshape(4, PAIR, KEYS)
            dq = join_heads(dot(ds, k), masks) * SCALE
            dk = dot(ds, q4, ((0,), (0,))) * SCALE
            dv = dot(p.astype(BF16), do4, ((0,), (0,)))
            dqkv_ref[rows, here] = dq.astype(BF16)
            dqkv_ref[rows, D + g * 128 : D + (g + 1) * 128] = dk[:PAIR].astype(BF16)
            dqkv_ref[rows, 2 * D + g * 128 : 2 * D + (g + 1) * 128] = dv[:PAIR].astype(BF16)
        return 0

    lax.fori_loop(0, PAIRS, attend, 0)
    n1, rstd1 = normalised(x_ref[...].astype(F32))
    turned_ref[...] = (n1 * small_ref[0:1] + small_ref[2:3]).T.astype(BF16)

    def qkv_step(n, _):
        cols = pl.ds(pl.multiple_of(n * CHUNK, CHUNK), CHUNK)
        g_ref[:, cols] = dot(turned_ref[...], dqkv_ref[:, cols]).astype(BF16)
        return 0

    lax.fori_loop(0, 3 * D // CHUNK, qkv_step, 0)
    gsmall_ref[4:5] = jnp.sum(dqkv_ref[:, 0:D].astype(F32), 0, keepdims=True)
    gsmall_ref[5:6] = jnp.sum(dqkv_ref[:, 2 * D : 3 * D].astype(F32), 0, keepdims=True)
    du = dot(dqkv_ref[...], w_ref[:, QKV0 : QKV0 + 3 * D], ((1,), (1,)))
    n1, rstd1 = normalised(x_ref[...].astype(F32))
    gsmall_ref[0:1] = jnp.sum(du * n1, 0, keepdims=True)
    gsmall_ref[2:3] = jnp.sum(du, 0, keepdims=True)
    z = du * small_ref[0:1]
    zm = jnp.mean(z, -1, keepdims=True)
    zn = jnp.mean(z * n1, -1, keepdims=True)
    dx = (du_ref[...] + rstd1 * (z - zm - n1 * zn)).astype(BF16)
    for b in range(IMGS):
        own = dx[b * IMG_ROWS : (b + 1) * IMG_ROWS]
        out_ref[b] = dot(back_ref[...], own).astype(BF16)
        if turned:
            next_ref[b * IMG_ROWS : (b + 1) * IMG_ROWS] = dot(turn_ref[...], own).astype(BF16)


def shaped(shape, dtype):
    return jax.ShapeDtypeStruct(shape, dtype)


def whole(shape):
    return pl.BlockSpec(shape, lambda *_: (0,) * len(shape))


def packed_block(layer):
    return pl.BlockSpec((D, PACKED), lambda *_: (layer, 0))


def run_forward(layer, turned, x, packed, small, qbias, hbias, rel, mask, back, turn):
    saved = [
        shaped((KROWS, 3 * D), BF16),
        shaped((ROWS, D), BF16),
        shaped((ROWS, D), F32),
        shaped((ROWS, FF), BF16),
        shaped((ROWS, FF), BF16),
        shaped((IMGS, OUT_ROWS, D), BF16),
    ]
    if turned:
        saved.append(shaped((ROWS, D), BF16))
    operands = (x, packed, small, qbias, hbias, rel, mask, back, turn)
    specs = [whole(a.shape) for a in operands]
    specs[1] = packed_block(layer)
    return pl.pallas_call(
        functools.partial(forward_kernel, turned),
        grid=(1,),
        out_shape=saved,
        in_specs=specs,
        out_specs=[whole(a.shape) for a in saved],
        scratch_shapes=[pltpu.VMEM((ROWS, D), BF16), pltpu.VMEM((ROWS, D), F32)],
        compiler_params=pltpu.CompilerParams(vmem_limit_bytes=VMEM_LIMIT),
        cost_estimate=pl.CostEstimate(
            flops=2 * ROWS * D * PACKED, bytes_accessed=16 << 20, transcendentals=2 * ROWS * FF
        ),
        name="forward_layer",
    )(*operands)


def run_backward(layer, turned, dy, x, saved, packed, small, rel, mask, back, turn):
    results = [
        shaped((D, PACKED), BF16),
        shaped((8, D), F32),
        shaped((1, FF), F32),
        shaped((16, PAIR, KEYS), F32),
        shaped((IMGS, OUT_ROWS, D), BF16),
    ]
    if turned:
        results.append(shaped((ROWS, D), BF16))
    operands = (dy, x, *saved, packed, small, rel, mask, back, turn)
    specs = [whole(a.shape) for a in operands]
    specs[7] = packed_block(layer)
    return pl.pallas_call(
        functools.partial(backward_kernel, turned),
        grid=(1,),
        out_shape=results,
        in_specs=specs,
        out_specs=[whole(a.shape) for a in results],
        scratch_shapes=[
            pltpu.VMEM((ROWS, D), BF16),
            pltpu.VMEM((D, ROWS), BF16),
            pltpu.VMEM((ROWS, CHUNK), BF16),
            pltpu.VMEM((ROWS, D), F32),
            pltpu.VMEM((ROWS, 3 * D), BF16),
            pltpu.VMEM((ROWS, D), BF16),
        ],
        compiler_params=pltpu.CompilerParams(vmem_limit_bytes=VMEM_LIMIT),
        cost_estimate=pl.CostEstimate(
            flops=4 * ROWS * D * PACKED, bytes_accessed=24 << 20, transcendentals=ROWS * FF
        ),
        name="backward_layer",
    )(*operands)


def block_pair(blocks, fill):
    lead = blocks.shape[:-3]
    none = [(0, 0)] * len(lead)
    pad_rows = [(0, WPAD - WTOK)]
    first = jnp.pad(blocks[..., 0, :, :], none + pad_rows + [(0, KEYS - WTOK)], constant_values=fill)
    second = jnp.pad(
        blocks[..., 1, :, :], none + pad_rows + [(WPAD, KEYS - WTOK - WPAD)], constant_values=fill
    )
    return jnp.concatenate([first, second], axis=-2)


def on_device(
    images, cotangent, micro_order, region_ids, rel_index, qkv_weight, proj_weight, up_weight,
    down_weight, bias_table, norm_gains, offsets, hidden_bias,
):
    section = lax.axis_index("pipe")
    first_section = section == 0
    both = ("pipe", "shard")
    shards = lax.axis_size("shard")

    mine = jnp.concatenate(
        [qkv_weight[0], proj_weight[0], up_weight[0]]
        + [down_weight[0, k * 128 : (k + 1) * 128] for k in range(4)],
        axis=1,
    )
    packed = lax.all_gather(mine, both, axis=0, tiled=True)
    table_rows = bias_table.shape[1]
    table = jnp.pad(bias_table[0].T, ((0, 0), (0, RELS_PAD - table_rows))).reshape(8, 128)
    tiny = jnp.concatenate(
        [norm_gains[0], offsets[0], hidden_bias[0].reshape(4, 128), table, jnp.zeros((12, 128), BF16)]
    )
    tiny = lax.all_gather(tiny, both, axis=0).reshape(2, shards, 32, 128)
    small = tiny[:, :, :8].transpose(0, 2, 1, 3).reshape(2, 8, D).astype(F32)
    hbias = tiny[:, :, 8:12].reshape(2, 1, FF).astype(F32)
    tables = tiny[:, :, 12:20].reshape(2 * 16, RELS_PAD)
    qbias = jnp.concatenate([small[:, 4:5], jnp.zeros((2, 1, D), F32), small[:, 5:6]], axis=2)

    inside = np.zeros((2, WTOK, WTOK), np.int32)
    rel_pair = block_pair(jnp.broadcast_to(rel_index, inside.shape), -1)
    one_hot = (
        lax.broadcasted_iota(jnp.int32, (RELS_PAD, PAIR * KEYS), 0) == rel_pair.reshape(1, -1)
    ).astype(BF16)
    rel = jnp.dot(tables, one_hot, preferred_element_type=F32).astype(BF16)
    rel = rel.reshape(2, 16, PAIR, KEYS)
    places = window_places(0)
    win_tokens = np.zeros((4, WTOK), np.int64)
    win_tokens[places // WPAD, places % WPAD] = np.arange(TOK)
    regions = region_ids.reshape(2, WIN, 2, WIN).transpose(0, 2, 1, 3).reshape(2, 2, WTOK)
    apart = jnp.where(regions[..., :, None] == regions[..., None, :], 0.0, -1e9).astype(F32)
    mask1 = block_pair(apart, BLOCKED)
    mask0 = block_pair(jnp.zeros((2, 2, WTOK, WTOK), F32), BLOCKED)

    slot_order = micro_order[0]
    first_slot = section * IMGS
    own_slots = lax.dynamic_slice(slot_order, (first_slot,), (IMGS,))
    order0 = jnp.asarray(order_matrix(0), BF16)
    order1 = jnp.asarray(order_matrix(SHIFT), BF16)
    back0 = jnp.asarray(back_matrix(0), BF16)
    back1 = jnp.asarray(back_matrix(SHIFT), BF16)
    turn01 = jnp.asarray(turn_matrix(0, SHIFT), BF16)
    turn10 = jnp.asarray(turn_matrix(SHIFT, 0), BF16)
    pictures = jnp.take(images, own_slots, axis=0)
    x0 = jnp.einsum("rt,btd->brd", order0, pictures, preferred_element_type=F32).astype(BF16)
    x0 = x0.reshape(ROWS, D)
    target = lax.dynamic_slice(cotangent, (first_slot, 0, 0), (IMGS, TOK, D))
    dy1 = jnp.einsum("rt,btd->brd", order1, target, preferred_element_type=F32).astype(BF16)
    dy1 = dy1.reshape(ROWS, D)

    *saved0, y0, x1 = run_forward(
        0, True, x0, packed, small[0], qbias[0], hbias[0], rel[0], mask0, back0, turn01
    )
    *saved1, y1 = run_forward(
        1, False, x1, packed, small[1], qbias[1], hbias[1], rel[1], mask1, back1, turn10
    )
    swap = [(0, 1), (1, 0)]
    y_keep = jnp.where(first_section, y0, y1)
    y_come = lax.ppermute(jnp.where(first_section, y1, y0), "pipe", swap)

    g1, gsmall1, ghidden1, gbias1, dx1, dy0 = run_backward(
        1, True, dy1, x1, saved1, packed, small[1], rel[1], mask1, back1, turn10
    )
    g0, gsmall0, ghidden0, gbias0, dx0 = run_backward(
        0, False, dy0, x0, saved0, packed, small[0], rel[0], mask0, back0, turn01
    )
    dx_keep = jnp.where(first_section, dx0, dx1)
    dx_come = lax.ppermute(jnp.where(first_section, dx1, dx0), "pipe", swap)

    def in_slots(keep, come):
        low = jnp.where(first_section, keep, come)
        high = jnp.where(first_section, come, keep)
        return jnp.concatenate([low, high], axis=0)[:, :TOK]

    layer_out = in_slots(y_keep, y_come)
    dx_slots = in_slots(dx_keep, dx_come)
    slots = jnp.arange(2 * IMGS, dtype=jnp.int32)
    inverse = jnp.sum(jnp.where(slot_order[:, None] == slots[None, :], slots[:, None], 0), axis=0)
    picks = jnp.where(first_section, inverse, slots)
    input_grad = jnp.take(dx_slots, picks, axis=0).astype(F32)

    everyone = ("pipe", "shard", "rep")
    big = jnp.concatenate([g0, g1], axis=0)
    share = reduce_big(big)
    gsmall = jnp.stack([gsmall0, gsmall1])
    ghidden = jnp.stack([ghidden0, ghidden1]).reshape(2, FF)
    gbias = jnp.stack([gbias0, gbias1])
    gbias = gbias[:, :, :WTOK, :WTOK] + gbias[:, :, WPAD : WPAD + WTOK, WPAD : WPAD + WTOK]
    rel_hot = (
        rel_index.reshape(1, -1) == jnp.arange(table_rows, dtype=jnp.int32)[:, None]
    ).astype(F32)
    gtable = jnp.einsum(
        "nr,hr->nh", rel_hot, gbias.reshape(32, WTOK * WTOK), precision=lax.Precision.HIGHEST
    )
    flat = jnp.concatenate([gsmall.reshape(-1), ghidden.reshape(-1), gtable.reshape(-1)])
    flat = lax.psum(flat, everyone)
    shard = lax.axis_index("shard")
    cut_small, cut_hidden = 2 * 8 * D, 2 * 8 * D + 2 * FF
    gsmall = lax.dynamic_slice(
        flat[:cut_small].reshape(2, 8, D), (section, 0, shard * 128), (1, 8, 128)
    )
    ghidden = lax.dynamic_slice(flat[cut_small:cut_hidden].reshape(2, FF), (section, shard * D), (1, D))
    gtable = lax.dynamic_slice(
        flat[cut_hidden:].reshape(table_rows, 32), (0, section * 16 + shard * 4), (table_rows, 4)
    )[None]
    down = jnp.concatenate(
        [share[:, DOWN0 + k * D : DOWN0 + (k + 1) * D] for k in range(4)], axis=0
    )
    return (
        layer_out[None],
        input_grad[None],
        share[None, :, QKV0:PROJ0].astype(F32),
        share[None, :, PROJ0:UP0].astype(F32),
        share[None, :, UP0:DOWN0].astype(F32),
        down[None].astype(F32),
        gtable,
        gsmall[:, 0:2],
        gsmall[:, 2:8],
        ghidden,
    )


def reduce_big(big):
    share = lax.psum_scatter(big, ("pipe", "shard"), scatter_dimension=0, tiled=True)
    return lax.psum(share, "rep")


def solution(mesh):
    rows = P(("shard", "rep"), None, None)
    split = P("pipe", "shard", None)
    lanes = P("pipe", None, "shard")
    return jax.shard_map(
        on_device,
        mesh=mesh,
        in_specs=(
            rows, rows, P(("shard", "rep"), None), P(), P(),
            split, split, split, split, lanes, lanes, lanes, P("pipe", "shard"),
        ),
        out_specs=(
            P("pipe", ("shard", "rep"), None, None), P("pipe", ("shard", "rep"), None, None),
            split, split, split, split, lanes, lanes, lanes, P("pipe", "shard"),
        ),
        check_vma=False,
    )
```

time: 1600 us -> 622 us (0.39)
  waiting for transfers between devices: 866 us -> 450 us
  local copies, waits for them, and re-layouts: 240 us -> 22.8 us
  matrix products: 204 us -> 5.79 us
  blocking collectives: 129 us -> 14.2 us
  Pallas kernels: 0 us -> 91.9 us
  other arithmetic: 101 us -> 21.4 us
  starting transfers between devices: 23.9 us -> 0.71 us
    reduce_scatter x20 -> x1, waiting for transfers between devices: 519 us -> 125 us  [reduce_big(): lax.psum_scatter(big, ('pipe', 'shard'), scatter_dimension=0, tiled=True)]
    unnamed x44 -> x4, waiting for transfers between devices: 246 us -> 0.07 us
    dot_general x91 -> x4, matrix products: 188 us -> 5.79 us  [the longest x1 2.66 us: on_device(): rel = jnp.dot(tables, one_hot, preferred_element_type=F32).astype(BF16)]
    psum x1 -> x2, waiting for transfers between devices: 67.6 us -> 221 us  [the longest x1 139 us: on_device(): flat = lax.psum(flat, everyone)]
    all_gather x3 -> x1, waiting for transfers between devices: 0.7 us -> 103 us  [on_device(): packed = lax.all_gather(mine, both, axis=0, tiled=True)]
    pallas_call x0 -> x4, Pallas kernels: none -> 91.9 us  [the longest x2 54.5 us: run_backward(): pl.pallas_call(functools.partial(backward_kernel, turned), grid=(1,), out...]
    convert_element_type x30 -> x0, local copies, waits for them, and re-layouts: 83 us -> none  [the longest x15 60 us: layer_backward(): projected_gradient = jnp.stack([d_queries, d_keys, d_values], 2).reshape(...]
    psum x1 -> x0, blocking collectives: 76.6 us -> none  [on_device(): lax.psum(shares[4].astype(jnp.bfloat16), 'rep').astype(jnp.float32)]
  transfers between devices with their start and end apart: 42 -> 6, of which waited for: 34 -> 4; matrix products, arithmetic and copies ran while one was open for 21% -> 5% of each run, Pallas kernels for 0% -> 0%
where the time goes in v1:
time: 622 us; the launch traced here: 621 us
  waiting for transfers between devices  450 us (72%)
  Pallas kernels  91.9 us (15%)
  local copies, waits for them, and re-layouts  22.8 us (4%)
  other arithmetic  21.4 us (3%)
  between operations  14.4 us (2%)
  blocking collectives  14.2 us (2%)
    psum x1, waiting for transfers between devices, on_device(): flat = lax.psum(flat, everyone)  139 us
    reduce_scatter x1, waiting for transfers between devices, reduce_big(): lax.psum_scatter(big, ('pipe', 'shard'), scatter_dimension=0, tiled=True)  125 us
    all_gather x1, waiting for transfers between devices, on_device(): packed = lax.all_gather(mine, both, axis=0, tiled=True)  103 us
    psum x1, waiting for transfers between devices, reduce_big(): return lax.psum(share, 'rep')  82.5 us
    pallas_call x2, Pallas kernels, run_backward(): pl.pallas_call(functools.partial(backward_kernel, turned), grid=(1,), out...  54.5 us
    pallas_call x2, Pallas kernels, run_forward(): pl.pallas_call(functools.partial(forward_kernel, turned), grid=(1,), out_...  37.4 us
    all_gather x1, blocking collectives, on_device(): tiny = lax.all_gather(tiny, both, axis=0).reshape(2, shards, 32, 128)  14.2 us
  transfers between devices with their start and end apart: 6, of which 4 were waited for; matrix products, arithmetic and copies ran while one was open for 5% of the time, Pallas kernels for 0%

profile of v1, /device:TPU:0, one launch (start us, length us, event | category | flops | bytes accessed | tf_op | source)
XLA Modules:
  0.0 621.0 jit_solution(15320041955608759121)
XLA Ops:
  7.2 1.1 bitcast_dynamic-update-slice_fusion.1
  8.4 0.9 bitcast_dynamic-update-slice_fusion.6
  9.4 1.1 bitcast_dynamic-update-slice_fusion
  10.6 1.1 copy-done.2
  12.1 14.2 %all-gather = bf16[256,128]{1,0:T(8,128)(2,1)S(1)} all-gather(bf16[32,128]{1,0:T(8,128)(2,1)S(1)} %concatenate.49), channel_id=2, replica_groups=mesh['pipe'=2,'shard'=4,'rep'=16] {'pipe','shard'}, dimensions={0}, use_global_device_ids=true | all-gather | bytes 73728 | tf_op jit(solution)/shard_map/all_gather | solution.py:386
  26.4 2.7 convolution_convert_fusion
  29.2 0.8 copy.67
  30.0 0.8 copy.68
  31.1 3.6 gather_fusion
  38.6 1.1 convolution_convert_fusion.2
  39.7 1.1 convolution_convert_fusion.1
  41.4 103.2 %all-gather.3.cloned.1.call-done.w_ref = bf16[1024,6144]{1,0:T(8,128)(2,1)} async-done(((bf16[128,6144]{1,0:T(8,128)(2,1)}), bf16[1024,6144]{1,0:T(8,128)(2,1)}) %all-gather.3.cloned.1.call-update) | async-done | bytes 12582928 | tf_op jit(solution)/shard_map/all_gather | solution.py:380
  144.6 18.9 %forward_layer.2 = (bf16[464,1536]{1,0:T(8,128)(2,1)}, bf16[448,512]{1,0:T(8,128)(2,1)}, f32[448,512]{1,0:T(8,128)}, bf16[448,2048]{1,0:T(8,128)(2,1)}, bf16[448...) custom-call(bf16[448,512]{1,0:T(8,128)(2,1)} %bitcast.122, ...), custom_call_target="tpu_custom_call" | custom-call | flops 2818572288 | bytes 16777216 | tf_op jit(solution)/shard_map/forward_layer/pallas_call | solution.py:305
  163.5 18.5 %forward_layer.3 = (bf16[464,1536]{1,0:T(8,128)(2,1)}, bf16[448,512]{1,0:T(8,128)(2,1)}, f32[448,512]{1,0:T(8,128)}, bf16[448,2048]{1,0:T(8,128)(2,1)}, bf16[448...) custom-call(bf16[448,512]{1,0:T(8,128)(2,1)} %get-tuple-element.35.x_ref, ...), custom_call_target="tpu_custom_call" | custom-call | flops 2818572288 | bytes 16777216 | tf_op jit(solution)/shard_map/forward_layer/pallas_call | solution.py:305
  182.0 27.4 %backward_layer.2 = (bf16[512,6144]{1,0:T(8,128)(2,1)}, f32[8,512]{1,0:T(8,128)}, f32[1,2048]{1,0:T(1,128)}, f32[16,112,128]{2,1,0:T(8,128)}, bf16[2,208,512]{2,1,0:T(8,128)(2,1)}, /*index=5*/bf16[448,512]{1,0:T(8,128)(2,1)}) custom-call(bf16[448,512]{1,0:T(8,128)(2,1)} %bitcast.126, bf16[448,512]{1,0:T(8,128)(2,1)} %get-tuple-element.35.x_ref, ...), custom_call_target="tpu_custom_call" | custom-call | flops 5637144576 | bytes 25165824 | tf_op jit(solution)/shard_map/backward_layer/pallas_call | solution.py:333
  209.4 27.1 %backward_layer.3 = (bf16[512,6144]{1,0:T(8,128)(2,1)}, f32[8,512]{1,0:T(8,128)}, f32[1,2048]{1,0:T(1,128)}, f32[16,112,128]{2,1,0:T(8,128)}, bf16[2,208,512]{2,1,0:T(8,128)(2,1)}) custom-call(bf16[448,512]{1,0:T(8,128)(2,1)} %get-tuple-element.42.dy_ref, bf16[448,512]{1,0:T(8,128)(2,1)} %bitcast.123, bf16[464,1536]{1,0:T(8,128)(2,1)} %get-tuple-element.43.qkv_ref, ...), custom_call_target="tpu_custom_call" | custom-call | flops 5637144576 | bytes 25165824 | tf_op jit(solution)/shard_map/backward_layer/pallas_call | solution.py:333
  236.5 10.5 %pad_maximum_fusion = bf16[1024,6144]{1,0:T(8,128)(2,1)} fusion(bf16[512,6144]{1,0:T(8,128)(2,1)} %get-tuple-element.51, bf16[512,6144]{1,0:T(8,128)(2,1)} %get-tuple-element.50), kind=kLoop, calls=%fused_computation.4 | loop fusion | flops 25165824 | bytes 25165824 | tf_op jit(solution)/shard_map/concatenate | solution.py:455
  247.3 0.9 copy-done.8
  248.1 1.5 fusion.3
  250.0 0.9 fusion.1
  252.1 125.2 %reduce-scatter.2.cloned.1.call-done = bf16[128,6144]{1,0:T(8,128)(2,1)} async-done(((bf16[1024,6144]{1,0:T(8,128)(2,1)}), bf16[128,6144]{1,0:T(8,128)(2,1)}) %reduce-scatter.2.cloned.1.call-update) | async-done | bytes 1572880 | tf_op jit(solution)/shard_map/reduce_scatter | solution.py:496
  377.4 0.8 broadcast_select_fusion.3
  378.5 138.9 %all-reduce.12.cloned.1.call-done = f32[17696]{0:T(1024)} async-done(((f32[17696]{0:T(1024)}), f32[17696]{0:T(1024)}) %all-reduce.12.cloned.1.call-update) | async-done | bytes 70800 | tf_op jit(solution)/shard_map/psum | solution.py:468
  517.3 0.7 slice.188
  518.2 0.8 slice.189
  522.4 1.3 copy.60
  524.7 2.2 copy.61
  526.9 82.5 %all-reduce.10.cloned.1.call-done = bf16[128,6144]{1,0:T(8,128)(2,1)} async-done(((bf16[128,6144]{1,0:T(8,128)(2,1)}), bf16[128,6144]{1,0:T(8,128)(2,1)}) %all-reduce.10.cloned.1.call-update) | async-done | bytes 1572880 | tf_op jit(solution)/shard_map/psum | solution.py:497
  609.3 2.0 slice_bitcast_fusion.7
  611.4 1.1 maximum_convert_fusion
  612.5 1.0 fusion.10
  613.4 1.1 fusion.7
  (121 shorter events, 11.8 us)
Async XLA Ops:
  7.2 23.9 %copy-start = (bf16[4,196,512]{2,0,1:T(4,128)(2,1)S(1)}, bf16[4,196,512]{2,0,1:T(4,128)(2,1)}, u32[]{:S(2)}) copy-start(bf16[4,196,512]{2,0,1:T(4,128)(2,1)} %param.19) | copy-start | bytes 2408452
  7.2 3.3 copy-start.9
  7.2 137.4 %all-gather.3.cloned.1.call-start = ((), (), s32[]{:S(2)}) async-start(), calls=%async_computation.1 | async-start | bytes 14155776 | tf_op jit(solution)/shard_map/all_gather | solution.py:380
  9.3 2.5 copy-start.20
  9.3 2.5 copy-start.19
  9.3 2.5 copy-start.18
  9.3 2.5 copy-start.22
  10.5 15.9 %copy-start.11 = (s32[49,49]{1,0:T(8,128)S(1)}, s32[49,49]{1,0:T(8,128)}, u32[]{:S(2)}) copy-start(s32[49,49]{1,0:T(8,128)} %param.23) | copy-start | bytes 28816
  10.6 1.1 copy-start.2
  11.7 365.7 %reduce-scatter.2.cloned.1.call-start = ((), (), s32[]{:S(2)}) async-start(), calls=%async_computation.2 | async-start | bytes 14155776 | tf_op jit(solution)/shard_map/reduce_scatter | solution.py:496
  29.1 1.8 copy-start.21
  29.1 2.0 copy-start.23
  31.1 5.3 copy-start.10
  34.8 3.8 copy-start.13
  35.6 4.0 copy-start.12
  247.0 1.2 copy-start.8
  247.0 270.4 %all-reduce.12.cloned.1.call-start = ((), (), s32[]{:S(2)}) async-start(), calls=%async_computation.4 | async-start | bytes 147456 | tf_op jit(solution)/shard_map/psum | solution.py:468
  249.6 1.3 copy-start.14
  249.6 1.3 copy-start.15
  249.6 1.4 copy-start.16
  249.6 1.4 copy-start.17
  249.7 2.1 copy-start.3
  249.7 2.1 copy-start.5
  250.9 126.5 %copy-start.4 = (bf16[2,208,512]{2,1,0:T(8,128)(2,1)S(1)}, bf16[2,208,512]{2,1,0:T(8,128)(2,1)}, u32[]{:S(2)}) copy-start(bf16[2,208,512]{2,1,0:T(8,128)(2,1)} %get-tuple-element.49) | copy-start | bytes 1277956
  251.0 126.5 %copy-start.6 = (bf16[2,208,512]{2,1,0:T(8,128)(2,1)S(1)}, bf16[2,208,512]{2,1,0:T(8,128)(2,1)}, u32[]{:S(2)}) copy-start(bf16[2,208,512]{2,1,0:T(8,128)(2,1)} %get-tuple-element.48) | copy-start | bytes 1277956
  251.7 357.6 %all-reduce.10.cloned.1.call-start = ((), (), s32[]{:S(2)}) async-start(), calls=%async_computation.3 | async-start | bytes 3145728 | tf_op jit(solution)/shard_map/psum | solution.py:497
  251.8 270.4 %collective-permute-start = (bf16[2,208,512]{2,1,0:T(8,128)(2,1)S(1)}, bf16[2,208,512]{2,1,0:T(8,128)(2,1)S(1)}, u32[]{:S(2)}, u32[]{:S(2)}) collective-permute-start(bf16[2,208,512]{2,1,0:T(8,128)(2,1)S(1)} %broadcast_select_fusion.7), channel_id=1, source_target_pairs={{0,64},{64,0},{1,65},{65,1},{2,66},{66,2},{3,67},{67,3},{4,68},{68... | collective-permute-start | bytes 1277960 | tf_op jit(solution)/shard_map/ppermute | solution.py:431
  378.2 145.5 %collective-permute-start.1 = (bf16[2,208,512]{2,1,0:T(8,128)(2,1)}, bf16[2,208,512]{2,1,0:T(8,128)(2,1)S(1)}, u32[]{:S(2)}, u32[]{:S(2)}) collective-permute-start(bf16[2,208,512]{2,1,0:T(8,128)(2,1)} %broadcast_select_fusion.3), channel_id=1, source_target_pairs={{0,64},{64,0},{1,65},{65,1},{2,66},{66,2},{3,67},{67,3},{4,68},{68... | collective-permute-start | bytes 1277960 | tf_op jit(solution)/shard_map/ppermute | solution.py:440
  609.3 3.1 copy-start.7
  611.4 3.1 copy-start.1
Sparse Core Ops, SparseCore 0:
  11.8 132.6 all-gather.2
  247.1 130.2 reduce-scatter.1
  382.7 134.5 all-reduce.11
  520.9 88.3 all-reduce.9

commit v2 on v1

v2 whole, which is shorter than its diff:
```python
import functools
import math

import jax
import jax.numpy as jnp
import numpy as np
from jax import lax
from jax.experimental import pallas as pl
from jax.experimental.pallas import tpu as pltpu
from jax.sharding import PartitionSpec as P

SIDE = 14
WIN = 7
SHIFT = 3
D = 512
FF = 2048
HEAD = 32
TOK = SIDE * SIDE
WTOK = WIN * WIN
WPAD = 56
PAIR = 2 * WPAD
IMG_ROWS = 4 * WPAD
IMGS = 2
ROWS = IMGS * IMG_ROWS
PAIRS = ROWS // PAIR
KEYS = 128
KROWS = ROWS + KEYS - PAIR
OUT_ROWS = 208
RELS_PAD = 256
QKV0, PROJ0, UP0, DOWN0, PACKED = 0, 1536, 2048, 4096, 6144
CHUNK = 256
SCALE = HEAD ** (-0.5)
BLOCKED = -1e30
VMEM_LIMIT = 64 * 1024 * 1024 - 1024
BF16 = jnp.bfloat16
F32 = jnp.float32


def window_places(shift):
    place = np.zeros((TOK,), np.int64)
    for wr in range(2):
        for wc in range(2):
            for i in range(WIN):
                for j in range(WIN):
                    a = (wr * WIN + i + shift) % SIDE
                    b = (wc * WIN + j + shift) % SIDE
                    place[a * SIDE + b] = (wr * 2 + wc) * WPAD + i * WIN + j
    return place


def order_matrix(shift):
    matrix = np.zeros((IMG_ROWS, TOK), np.float32)
    matrix[window_places(shift), np.arange(TOK)] = 1.0
    return matrix


def back_matrix(shift):
    matrix = np.zeros((OUT_ROWS, IMG_ROWS), np.float32)
    matrix[:TOK] = order_matrix(shift).T
    return matrix


def turn_matrix(from_shift, to_shift):
    return order_matrix(to_shift) @ order_matrix(from_shift).T


def dot(a, b, dims=((1,), (0,))):
    return lax.dot_general(a, b, (dims, ((), ())), preferred_element_type=F32)


def normalised(x):
    mean = jnp.mean(x, -1, keepdims=True)
    centred = x - mean
    rstd = lax.rsqrt(jnp.mean(centred * centred, -1, keepdims=True) + 1e-5)
    return centred * rstd, rstd


def head_masks(rows):
    lane = lax.broadcasted_iota(jnp.int32, (rows, 128), 1) // HEAD
    return [lane == h for h in range(4)]


def spread_heads(block, masks):
    zero = jnp.zeros_like(block)
    return jnp.concatenate([jnp.where(m, block, zero) for m in masks], axis=0)


def join_heads(stacked, masks):
    total = None
    for h, m in enumerate(masks):
        part = jnp.where(m, stacked[h * PAIR : (h + 1) * PAIR], 0.0)
        total = part if total is None else total + part
    return total


def probabilities(q4, k, rel_ref, mask_ref, i, g):
    s = dot(q4, k, ((1,), (1,))) * SCALE
    bias = rel_ref[pl.ds(g * 4, 4)].astype(F32) + mask_ref[lax.rem(i, 2)][None]
    s = s + bias.reshape(4 * PAIR, KEYS)
    e = jnp.exp(s - jnp.max(s, -1, keepdims=True))
    return e / jnp.sum(e, -1, keepdims=True)


def down_chunk(w_ref, c):
    row = pl.multiple_of((c // 2) * 128, 128)
    col = pl.multiple_of(DOWN0 + (c % 2) * 1024, 128)
    first = w_ref[pl.ds(row, 128), pl.ds(col, D)]
    second = w_ref[pl.ds(row, 128), pl.ds(col + D, D)]
    return jnp.concatenate([first, second], axis=0)


MESH = pl.DeviceIdType.MESH
STREAMS = ((2048, 4096, "xz"), (4096, 6144, "zx"), (0, 1024, "xz"), (1024, 2048, "zx"))
LATE = (2, 3)
TINY_ROWS = 24
SMALL_ROWS = 24


def here():
    pipe, shard, rep = lax.axis_index("pipe"), lax.axis_index("shard"), lax.axis_index("rep")
    return {"y": (shard // 2) * 2 + pipe, "core": shard % 2, "z": rep // 4, "x": rep % 4}


def device_at(place):
    return {
        "pipe": place["y"] % 2,
        "shard": (place["y"] // 2) * 2 + place["core"],
        "rep": place["z"] * 4 + place["x"],
    }


def moved(place, axis, steps):
    size = 2 if axis == "core" else 4
    return {**place, axis: (place[axis] + steps) % size}


def block_index(y, core):
    return (y % 2) * 4 + (y // 2) * 2 + core


class Copies:
    def __init__(self, send_sem, recv_sem):
        self.send_sem, self.recv_sem, self.count, self.started = send_sem, recv_sem, 0, []

    def start(self, src, dst, place):
        copy = pltpu.make_async_remote_copy(
            src_ref=src, dst_ref=dst, send_sem=self.send_sem.at[self.count],
            recv_sem=self.recv_sem.at[self.count], device_id=device_at(place), device_id_type=MESH,
        )
        copy.start()
        self.count += 1
        self.started.append(copy)
        return copy

    def finish(self):
        for copy in self.started:
            copy.wait_send()


def greet(places):
    barrier = pltpu.get_barrier_semaphore()
    for place in places:
        pl.semaphore_signal(barrier, inc=1, device_id=device_at(place), device_id_type=MESH)
    pl.semaphore_wait(barrier, len(places))


def nothing():
    pass


def forward_body(params, saved, x_ref, low_ref, acc_ref, after_attend=nothing):
    w_ref, small_ref, qbias_ref, hbias_ref, rel_ref, mask_ref = params
    qkv_ref, o_ref, r_ref, act_ref, slope_ref = saved
    n1, _ = normalised(x_ref[...].astype(F32))
    low_ref[...] = (n1 * small_ref[0:1] + small_ref[2:3]).astype(BF16)
    qkv_ref[ROWS:, :] = jnp.zeros((KROWS - ROWS, 3 * D), BF16)

    def qkv_step(n, _):
        cols = pl.ds(pl.multiple_of(n * CHUNK, CHUNK), CHUNK)
        part = dot(low_ref[...], w_ref[:, cols]) + qbias_ref[:, cols]
        qkv_ref[0:ROWS, cols] = part.astype(BF16)
        return 0

    lax.fori_loop(0, 3 * D // CHUNK, qkv_step, 0)
    masks = head_masks(PAIR)

    def attend(i, _):
        rows = pl.ds(pl.multiple_of(i * PAIR, 16), PAIR)
        keys = pl.ds(pl.multiple_of(i * PAIR, 16), KEYS)
        for g in range(4):
            q = qkv_ref[rows, g * 128 : (g + 1) * 128]
            k = qkv_ref[keys, D + g * 128 : D + (g + 1) * 128]
            v = qkv_ref[keys, 2 * D + g * 128 : 2 * D + (g + 1) * 128]
            p = probabilities(spread_heads(q, masks), k, rel_ref, mask_ref, i, g)
            o4 = dot(p.astype(BF16), v)
            o_ref[rows, g * 128 : (g + 1) * 128] = join_heads(o4, masks).astype(BF16)
        return 0

    lax.fori_loop(0, PAIRS, attend, 0)
    after_attend()
    for n in range(D // CHUNK):
        cols = slice(n * CHUNK, (n + 1) * CHUNK)
        part = dot(o_ref[...], w_ref[:, PROJ0 + n * CHUNK : PROJ0 + (n + 1) * CHUNK])
        r_ref[:, cols] = x_ref[:, cols].astype(F32) + part + small_ref[6:7, cols]
    r = r_ref[...]
    n2, _ = normalised(r)
    low_ref[...] = (n2 * small_ref[1:2] + small_ref[3:4]).astype(BF16)
    acc_ref[...] = r + small_ref[7:8]

    def mlp(c, _):
        cols = pl.ds(pl.multiple_of(c * CHUNK, CHUNK), CHUNK)
        up = w_ref[:, pl.ds(pl.multiple_of(UP0 + c * CHUNK, CHUNK), CHUNK)]
        hid = dot(low_ref[...], up) + hbias_ref[:, cols]
        cdf = 0.5 * (1.0 + lax.erf(hid * math.sqrt(0.5)))
        act = (hid * cdf).astype(BF16)
        act_ref[:, cols] = act
        density = jnp.exp(-0.5 * hid * hid) * (1.0 / math.sqrt(2.0 * math.pi))
        slope_ref[:, cols] = (cdf + hid * density).astype(BF16)
        acc_ref[...] += dot(act, down_chunk(w_ref, c))
        return 0

    lax.fori_loop(0, FF // CHUNK, mlp, 0)
    return acc_ref[...].astype(BF16)


def backward_body(
    params, saved, x_ref, dy_ref, results, scratch,
    in_mlp=nothing, after_mlp=nothing, before_attend=nothing, after_attend=nothing, after_weights=nothing,
):
    w_ref, small_ref, _, _, rel_ref, mask_ref = params
    qkv_ref, o_ref, r_ref, act_ref, slope_ref = saved
    g_ref, gsmall_ref, ghidden_ref, gbias_ref = results
    low_ref, turned_ref, du_ref, dqkv_ref, do_ref = scratch

    def put(cols, value):
        for b in range(4):
            g_ref[b // 2, b % 2, :, cols] = value[b * 128 : (b + 1) * 128]

    n2, rstd2 = normalised(r_ref[...])
    turned_ref[...] = (n2 * small_ref[1:2] + small_ref[3:4]).T.astype(BF16)
    du_ref[...] = jnp.zeros_like(du_ref)

    def mlp(c, _):
        cols = pl.ds(pl.multiple_of(c * CHUNK, CHUNK), CHUNK)
        up_cols = pl.ds(pl.multiple_of(UP0 + c * CHUNK, CHUNK), CHUNK)
        dy = dy_ref[...]
        dact = dot(dy, down_chunk(w_ref, c), ((1,), (1,)))
        dhid = (dact * slope_ref[:, cols].astype(F32)).astype(BF16)
        ghidden_ref[:, cols] = jnp.sum(dhid.astype(F32), 0, keepdims=True)
        down = dot(act_ref[:, cols], dy, ((0,), (0,))).astype(BF16)
        block = c // 2
        col = pl.multiple_of(DOWN0 + (c % 2) * 1024, 128)
        g_ref[block // 2, block % 2, :, pl.ds(col, D)] = down[:128]
        g_ref[block // 2, block % 2, :, pl.ds(col + D, D)] = down[128:]
        put(up_cols, dot(turned_ref[...], dhid).astype(BF16))
        du_ref[...] += dot(dhid, w_ref[:, up_cols], ((1,), (1,)))
        return 0

    lax.fori_loop(0, FF // CHUNK // 2, mlp, 0)
    in_mlp()
    lax.fori_loop(FF // CHUNK // 2, FF // CHUNK, mlp, 0)
    after_mlp()
    dy = dy_ref[...].astype(F32)
    du2 = du_ref[...]
    n2, rstd2 = normalised(r_ref[...])
    z = du2 * small_ref[1:2]
    zm = jnp.mean(z, -1, keepdims=True)
    zn = jnp.mean(z * n2, -1, keepdims=True)
    dr = dy + rstd2 * (z - zm - n2 * zn)
    db = dr.astype(BF16)
    low_ref[...] = db
    gsmall_ref[1:2] = jnp.sum(du2 * n2, 0, keepdims=True)
    gsmall_ref[3:4] = jnp.sum(du2, 0, keepdims=True)
    gsmall_ref[6:7] = jnp.sum(db.astype(F32), 0, keepdims=True)
    gsmall_ref[7:8] = jnp.sum(dy, 0, keepdims=True)
    du_ref[...] = dr
    turned_ref[...] = o_ref[...].astype(F32).T.astype(BF16)
    for n in range(D // CHUNK):
        cols = slice(n * CHUNK, (n + 1) * CHUNK)
        put(
            slice(PROJ0 + n * CHUNK, PROJ0 + (n + 1) * CHUNK),
            dot(turned_ref[...], low_ref[:, cols]).astype(BF16),
        )
        rows_of = w_ref[n * CHUNK : (n + 1) * CHUNK, PROJ0 : PROJ0 + D]
        do_ref[:, cols] = dot(low_ref[...], rows_of, ((1,), (1,))).astype(BF16)
    before_attend()
    gbias_ref[...] = jnp.zeros_like(gbias_ref)
    masks = head_masks(PAIR)

    def attend(i, _):
        rows = pl.ds(pl.multiple_of(i * PAIR, 16), PAIR)
        keys = pl.ds(pl.multiple_of(i * PAIR, 16), KEYS)
        for g in range(4):
            here = slice(g * 128, (g + 1) * 128)
            k = qkv_ref[keys, D + g * 128 : D + (g + 1) * 128]
            v = qkv_ref[keys, 2 * D + g * 128 : 2 * D + (g + 1) * 128]
            q4 = spread_heads(qkv_ref[rows, here], masks)
            do4 = spread_heads(do_ref[rows, here], masks)
            p = probabilities(q4, k, rel_ref, mask_ref, i, g)
            dp = dot(do4, v, ((1,), (1,)))
            ds = (p * (dp - jnp.sum(dp * p, -1, keepdims=True))).astype(BF16)
            gbias_ref[g * 4 : (g + 1) * 4] += ds.astype(F32).reshape(4, PAIR, KEYS)
            dq = join_heads(dot(ds, k), masks) * SCALE
            dk = dot(ds, q4, ((0,), (0,))) * SCALE
            dv = dot(p.astype(BF16), do4, ((0,), (0,)))
            dqkv_ref[rows, here] = dq.astype(BF16)
            dqkv_ref[rows, D + g * 128 : D + (g + 1) * 128] = dk[:PAIR].astype(BF16)
            dqkv_ref[rows, 2 * D + g * 128 : 2 * D + (g + 1) * 128] = dv[:PAIR].astype(BF16)
        return 0

    lax.fori_loop(0, PAIRS, attend, 0)
    after_attend()
    n1, rstd1 = normalised(x_ref[...].astype(F32))
    turned_ref[...] = (n1 * small_ref[0:1] + small_ref[2:3]).T.astype(BF16)

    def qkv_step(n, _):
        cols = pl.ds(pl.multiple_of(n * CHUNK, CHUNK), CHUNK)
        put(cols, dot(turned_ref[...], dqkv_ref[:, cols]).astype(BF16))
        return 0

    lax.fori_loop(0, 3 * D // CHUNK, qkv_step, 0)
    after_weights()
    gsmall_ref[4:5] = jnp.sum(dqkv_ref[:, 0:D].astype(F32), 0, keepdims=True)
    gsmall_ref[5:6] = jnp.sum(dqkv_ref[:, 2 * D : 3 * D].astype(F32), 0, keepdims=True)
    du = dot(dqkv_ref[...], w_ref[:, QKV0 : QKV0 + 3 * D], ((1,), (1,)))
    n1, rstd1 = normalised(x_ref[...].astype(F32))
    gsmall_ref[0:1] = jnp.sum(du * n1, 0, keepdims=True)
    gsmall_ref[2:3] = jnp.sum(du, 0, keepdims=True)
    z = du * small_ref[0:1]
    zm = jnp.mean(z, -1, keepdims=True)
    zn = jnp.mean(z * n1, -1, keepdims=True)
    return (du_ref[...] + rstd1 * (z - zm - n1 * zn)).astype(BF16)


def table_rows_of(tables_ref, places_ref, rel_ref):
    rel_ref[...] = jnp.zeros_like(rel_ref)
    entry = lax.broadcasted_iota(jnp.int32, (RELS_PAD, KEYS), 0)
    tables = tables_ref[...].astype(BF16)

    def rows(n, _):
        for step in range(WIN):
            i = n * WIN + step
            hot = jnp.where(entry == places_ref[pl.ds(i, 1), :], 1.0, 0.0).astype(BF16)
            values = dot(tables, hot)
            rel_ref[:, i, :] = values
            rel_ref[:, i + WPAD, :] = pltpu.roll(values, WPAD, 1)
        return 0

    lax.fori_loop(0, WIN, rows, 0)


def table_sums(gbias_ref, places_ref):
    second = gbias_ref[:, WPAD:PAIR].reshape(16 * WPAD, KEYS)
    gbias_ref[:, 0:WPAD] += pltpu.roll(second, KEYS - WPAD, 1).reshape(16, WPAD, KEYS)
    entry = lax.broadcasted_iota(jnp.int32, (RELS_PAD, KEYS), 0)

    def rows(n, total):
        parts = []
        for step in range(WIN):
            i = n * WIN + step
            values = gbias_ref[:, i, :]
            high = values.astype(BF16)
            low = (values - high.astype(F32)).astype(BF16)
            hot = jnp.where(entry == places_ref[pl.ds(i, 1), :], 1.0, 0.0).astype(BF16)
            parts.append(dot(jnp.concatenate([high, low], axis=0), hot, ((1,), (1,))))
        return total + sum(parts)

    total = lax.fori_loop(0, WIN, rows, jnp.zeros((32, RELS_PAD), F32))
    return total[0:16] + total[16:32]


COPIES = 192


def piece_of(region):
    rows, cols = region
    return (pl.ds(rows[0], rows[1]), pl.ds(cols[0], cols[1]))


def cut(region, axis, index):
    rows, cols = region
    if axis == "z":
        return ((pl.multiple_of(index * 32, 32), 32), cols)
    width = cols[1] // 4
    return (rows, (pl.multiple_of(cols[0] + index * width, 128), width))


def train_kernel(
    slots_ref, images_ref, cot_hbm, qkv_hbm, proj_hbm, up_hbm, down_hbm, tiny_ref, places_ref, mask_ref,
    order_ref, back_ref, turn_ref,
    y_hbm, dx_hbm, grad_hbm, sums_ref,
    w_ref, x_ref, qkv_ref, o_ref, r_ref, act_ref, slope_ref, g_ref, core_ref, land_a, land_b, land_y, fin_ref,
    rel_ref, gbias_ref, low_ref, turned_ref, du_ref, dqkv_ref, do_ref, dy_ref, cot_ref,
    y_ref, y_land, dx_ref, dx_land, tiny_land, tables_ref, small_ref, qbias_ref, hbias_ref,
    gsmall_ref, ghidden_ref, sums_in, sums_core, sums_own, sums_land,
    send_sem, recv_sem, local_sem, free_sem,
):
    me = here()
    pipe = me["y"] % 2
    copies = Copies(send_sem, recv_sem)
    partner = moved(me, "core", 1)
    peers = {axis: [moved(me, axis, k) for k in (1, 2, 3)] for axis in "yxz"}
    across = [moved(partner, "y", k) for k in (1, 2, 3)]

    def block_at(y):
        return pl.ds(pl.multiple_of(block_index(y, me["core"]) * 128, 128), 128)

    own = block_index(me["y"], me["core"])
    own_rows = block_at(me["y"])
    parts = [
        (qkv_hbm.at[0], QKV0, 3 * D), (proj_hbm.at[0], PROJ0, D), (up_hbm.at[0], UP0, FF),
    ] + [(down_hbm.at[0, k * 128 : (k + 1) * 128], DOWN0 + k * D, D) for k in range(4)]
    locals_in = []
    for n, (src, lo, width) in enumerate(parts):
        local = pltpu.make_async_copy(src, w_ref.at[own_rows, lo : lo + width], local_sem.at[n])
        local.start()
        locals_in.append(local)
    cot_copy = pltpu.make_async_copy(cot_hbm.at[pl.ds(pipe * IMGS, IMGS)], cot_ref, local_sem.at[7])
    cot_copy.start()
    greet([partner] + across + [place for axis in "yxz" for place in peers[axis]])
    for local in locals_in:
        local.wait()

    width = PACKED // 8

    def quarter(half, part, index):
        return (half * 64, 64), (pl.multiple_of(part * (PACKED // 2) + index * width, 128), width)

    def weight_piece(y, region):
        (r0, nr), cols = region
        start = pl.multiple_of(block_index(y, me["core"]) * 128 + r0, 64)
        return w_ref.at[pl.ds(start, nr), pl.ds(*cols)]

    first_base = copies.count
    for half in range(2):
        for k in (1, 2, 3):
            for part, axis in enumerate("xz"):
                piece = weight_piece(me["y"], quarter(half, part, me[axis]))
                copies.start(piece, piece, moved(me, "y", k))
    own_block = w_ref.at[own_rows]
    to_partner = {"own": copies.start(own_block, own_block, partner)}
    tiny_copies = [
        copies.start(tiny_ref, tiny_land.at[own], place) for place in [partner] + peers["y"] + across
    ]
    tiny_land[own] = tiny_ref[...]

    for b in range(IMGS):
        picture = images_ref[slots_ref[pipe * IMGS + b]]
        x_ref[0, b * IMG_ROWS : (b + 1) * IMG_ROWS] = dot(order_ref[0], picture).astype(BF16)
    cot_copy.wait()
    for b in range(IMGS):
        dy_ref[b * IMG_ROWS : (b + 1) * IMG_ROWS] = dot(order_ref[1], cot_ref[b]).astype(BF16)
    for copy in tiny_copies:
        copy.wait_recv()
    qbias_ref[...] = jnp.zeros_like(qbias_ref)
    for layer in range(2):
        for shard in range(4):
            rows = tiny_land[layer * 4 + shard]
            small_ref[layer, :, shard * 128 : (shard + 1) * 128] = rows[0:8, 0:128]
            for j in range(4):
                at = shard * 512 + j * 128
                hbias_ref[layer, :, at : at + 128] = rows[8 + j : 9 + j, 0:128]
                head = layer * 16 + shard * 4 + j
                tables_ref[head : head + 1] = rows[16 + j : 17 + j]
        qbias_ref[layer, :, 0:D] = small_ref[layer, 4:5]
        qbias_ref[layer, :, 2 * D : 3 * D] = small_ref[layer, 5:6]

    steps = [2 - pipe, 1 + 2 * pipe, 3 - pipe]
    seconds = {}

    def pass_on(slot):
        y = (me["y"] - steps[slot] + 4) % 4
        for half in range(2):
            for part, axis in enumerate("xz"):
                piece = weight_piece(y, quarter(half, part, me[axis]))
                index = first_base + half * 6 + (steps[slot] - 1) * 2 + part
                pltpu.make_async_remote_copy(
                    src_ref=piece, dst_ref=piece, send_sem=send_sem.at[index],
                    recv_sem=recv_sem.at[index], device_id=device_at(partner), device_id_type=MESH,
                ).wait_recv()
                for j in (1, 3, 2):
                    seconds[slot, half, part, j] = copies.start(piece, piece, moved(me, axis, j))

    def hand_over(slot):
        y = (me["y"] - steps[slot] + 4) % 4
        for half in range(2):
            for part in range(2):
                for j in (1, 3, 2):
                    seconds[slot, half, part, j].wait_recv()
            piece = weight_piece(y, ((half * 64, 64), (0, PACKED)))
            to_partner[slot, half] = copies.start(piece, piece, partner)

    pass_on(0)
    pass_on(1)
    table_rows_of(tables_ref, places_ref, rel_ref)
    hand_over(0)
    hand_over(1)
    pass_on(2)
    to_partner["own"].wait_recv()
    for slot in range(2):
        for half in range(2):
            to_partner[slot, half].wait_recv()

    def params(layer):
        return (
            w_ref.at[pl.ds(layer * D, D)], small_ref.at[layer], qbias_ref.at[layer], hbias_ref.at[layer],
            rel_ref.at[pl.ds(layer * 16, 16)], mask_ref.at[layer],
        )

    def saved(layer):
        return tuple(ref.at[layer] for ref in (qkv_ref, o_ref, r_ref, act_ref, slope_ref))

    def in_token_order(layer, value, out, turned):
        for b in range(IMGS):
            own_rows = value[b * IMG_ROWS : (b + 1) * IMG_ROWS]
            out[b] = dot(back_ref[layer], own_rows).astype(BF16)
            if turned is not None:
                turned[b * IMG_ROWS : (b + 1) * IMG_ROWS] = dot(turn_ref[layer], own_rows).astype(BF16)

    y0 = forward_body(params(0), saved(0), x_ref.at[0], low_ref, du_ref, lambda: hand_over(2))
    in_token_order(0, y0, y_ref.at[0], x_ref.at[1])
    for half in range(2):
        to_partner[2, half].wait_recv()
    y1 = forward_body(params(1), saved(1), x_ref.at[1], low_ref, du_ref)
    in_token_order(1, y1, y_ref.at[1], None)
    neighbour = {**me, "y": me["y"] + 1 - 2 * pipe}
    y_copy = copies.start(y_ref.at[1 - pipe], y_land, neighbour)
    keep_out = pltpu.make_async_copy(y_ref.at[pipe], y_hbm.at[pl.ds(pipe * IMGS, IMGS)], local_sem.at[0])
    keep_out.start()

    core_copies, sent, regions = {}, {}, {}

    def send_core(layer, streams):
        for t in streams:
            lo, hi, _ = STREAMS[t]
            core_copies[layer, t] = copies.start(
                g_ref.at[layer, :, 1 - me["core"], :, lo:hi], core_ref.at[:, :, lo:hi], partner
            )

    def add_core(layer, streams):
        for t in streams:
            lo, hi, _ = STREAMS[t]
            core_copies[layer, t].wait_recv()

            def one(n, _, lo=lo, hi=hi):
                half, rows = n // 4, pl.ds(pl.multiple_of((n % 4) * 32, 32), 32)
                mine = (layer, half, me["core"], rows, slice(lo, hi))
                total = g_ref[mine].astype(F32) + core_ref[half, rows, lo:hi].astype(F32)
                g_ref[mine] = total.astype(BF16)
                return 0

            lax.fori_loop(0, 8, one, 0)
            regions[layer, t] = ((0, 128), (lo, hi - lo))

    def send(layer, streams, stage):
        for t in streams:
            axis = STREAMS[t][2][stage]
            land = (land_a, land_b)[stage][t]
            region = regions[layer, t]
            sent[layer, t] = [
                copies.start(
                    g_ref.at[(layer, slice(None), me["core"]) + piece_of(cut(region, axis, (me[axis] + k) % 4))],
                    land.at[layer, k - 1], moved(me, axis, k),
                )
                for k in (1, 3, 2)
            ]
            regions[layer, t] = cut(region, axis, me[axis])

    def add(layer, streams, stage):
        for t in streams:
            for copy in sent[layer, t]:
                copy.wait_recv()
            land = (land_a, land_b)[stage][t]
            (r0, nr), cols = regions[layer, t]
            steps_of = nr // 32

            def one(n, _, land=land, r0=r0, cols=cols, steps_of=steps_of):
                half, row = n // steps_of, pl.multiple_of((n % steps_of) * 32, 32)
                at = (layer, half, me["core"], pl.ds(pl.multiple_of(r0 + row, 32), 32), pl.ds(*cols))
                total = g_ref[at].astype(F32)
                for k in range(3):
                    total = total + land[layer, k, half, pl.ds(row, 32), :].astype(F32)
                g_ref[at] = total.astype(BF16)
                return 0

            lax.fori_loop(0, 2 * steps_of, one, 0)

    def send_y(streams):
        for t in streams:
            piece = piece_of(regions[0, t])
            sent["y", t] = []
            for k in (1, 3, 2):
                to = (me["y"] + k) % 4
                sent["y", t].append(
                    copies.start(
                        g_ref.at[(to % 2, to // 2, me["core"]) + piece], land_y[t].at[k - 1], moved(me, "y", k)
                    )
                )

    def add_y(streams):
        for t in streams:
            for copy in sent["y", t]:
                copy.wait_recv()
            piece = piece_of(regions[0, t])
            total = g_ref[(pipe, me["y"] // 2, me["core"]) + piece].astype(F32)
            for k in range(3):
                total = total + land_y[t][k].astype(F32)
            fin_ref[piece] = total.astype(BF16)

    def spread(streams, level):
        for t in streams:
            if level == 1:
                for copy in sent["fin", t]:
                    copy.wait_recv()
            lo, hi, order = STREAMS[t]
            part = (hi - lo) // 4
            rows = pl.ds(pl.multiple_of(me["z"] * 32, 32), 32)
            cols = pl.ds(pl.multiple_of(lo + me["x"] * part, 128), part)
            if level == 1:
                if order[0] == "x":
                    cols = pl.ds(lo, hi - lo)
                else:
                    rows = pl.ds(0, 128)
            piece = fin_ref.at[rows, cols]
            sent["fin", t] = [copies.start(piece, piece, moved(me, order[level], k)) for k in (1, 3, 2)]

    late = LATE
    early = tuple(t for t in range(len(STREAMS)) if t not in late)

    def results(layer):
        return (g_ref.at[layer], gsmall_ref.at[layer], ghidden_ref.at[layer], gbias_ref.at[layer])

    scratch = (low_ref, turned_ref, du_ref, dqkv_ref, do_ref)

    def before_attend1():
        add_core(1, early)
        send(1, early, 0)

    dx1 = backward_body(
        params(1), saved(1), x_ref.at[1], dy_ref, results(1), scratch,
        after_mlp=lambda: send_core(1, early), before_attend=before_attend1,
        after_weights=lambda: send_core(1, late),
    )
    in_token_order(1, dx1, dx_ref.at[1], dy_ref)
    add_core(1, late)
    pl.semaphore_signal(free_sem, inc=1, device_id=device_at(partner), device_id_type=MESH)
    send(1, late, 0)

    def in_mlp0():
        add(1, early, 0)
        send(1, early, 1)

    def after_mlp0():
        pl.semaphore_wait(free_sem, 1)
        send_core(0, early)
        add(1, late, 0)
        send(1, late, 1)

    def before_attend0():
        add_core(0, early)
        send(0, early, 0)

    def after_weights0():
        send_core(0, late)
        add(1, early, 1)
        add(1, late, 1)

    dx0 = backward_body(
        params(0), saved(0), x_ref.at[0], dy_ref, results(0), scratch,
        in_mlp=in_mlp0, after_mlp=after_mlp0, before_attend=before_attend0, after_weights=after_weights0,
    )
    add_core(0, late)
    send(0, late, 0)
    in_token_order(0, dx0, dx_ref.at[0], None)
    dx_copy = copies.start(dx_ref.at[1 - pipe], dx_land, neighbour)
    dx_keep = pltpu.make_async_copy(dx_ref.at[pipe], dx_hbm.at[pl.ds(pipe * IMGS, IMGS)], local_sem.at[1])
    dx_keep.start()
    add(0, early, 0)
    send(0, early, 1)

    for layer in range(2):
        gtable = table_sums(gbias_ref.at[layer], places_ref)
        for shard in range(4):
            half, core = shard // 2, shard % 2
            y = half * 2 + layer
            sums_in[core, y] = jnp.zeros((SMALL_ROWS, RELS_PAD), F32)
            sums_in[core, y, 0:8, 0:128] = gsmall_ref[layer, :, shard * 128 : (shard + 1) * 128]
            for j in range(4):
                at = shard * 512 + j * 128
                sums_in[core, y, 8 + j : 9 + j, 0:128] = ghidden_ref[layer, :, at : at + 128]
            sums_in[core, y, 16:20] = gtable[shard * 4 : shard * 4 + 4]
    small_copy = copies.start(sums_in.at[1 - me["core"]], sums_core, partner)
    add(0, early, 1)
    send_y(early)
    add(0, late, 0)
    send(0, late, 1)
    small_copy.wait_recv()
    sums_own[0] = sums_in[me["core"]] + sums_core[...]
    small_sent = [
        copies.start(sums_own.at[0, (me["y"] + k) % 4], sums_land.at[0, k - 1], moved(me, "y", k))
        for k in (1, 3, 2)
    ]

    def add_small(stage):
        for copy in small_sent:
            copy.wait_recv()
        start = sums_own[0, me["y"]] if stage == 0 else sums_own[stage, 0]
        return start + sums_land[stage, 0] + sums_land[stage, 1] + sums_land[stage, 2]

    add_y(early)
    spread(early, 0)
    add(0, late, 1)
    send_y(late)
    for stage, axis in enumerate("xz", 1):
        sums_own[stage, 0] = add_small(stage - 1)
        small_sent = [
            copies.start(sums_own.at[stage, 0], sums_land.at[stage, k - 1], moved(me, axis, k))
            for k in (1, 3, 2)
        ]
        if stage == 1:
            spread(early, 1)
            add_y(late)
            spread(late, 0)
    spread(late, 1)
    sums_ref[...] = add_small(2)
    outs = []
    y_copy.wait_recv()
    dx_copy.wait_recv()
    for n, (src, dst) in enumerate(((y_land, y_hbm), (dx_land, dx_hbm)), 2):
        out = pltpu.make_async_copy(src, dst.at[pl.ds((1 - pipe) * IMGS, IMGS)], local_sem.at[n])
        out.start()
        outs.append(out)
    for t in early + late:
        for copy in sent["fin", t]:
            copy.wait_recv()
    grad_out = pltpu.make_async_copy(fin_ref, grad_hbm, local_sem.at[4])
    grad_out.start()
    for copy in [keep_out, dx_keep, grad_out] + outs:
        copy.wait()
    copies.finish()


def land_shapes(stage):
    shapes = []
    for lo, hi, order in STREAMS:
        done = order[: stage + 1]
        shape = (2, 3, 2, 32 if "z" in done else 128, (hi - lo) // (4 if "x" in done else 1))
        shapes.append(pltpu.VMEM(shape, BF16))
    return tuple(shapes)


def train(slots, images, cotangent, qkv, proj, up, down, tiny, places, mask, order, back, turn):
    anywhere = pl.BlockSpec(memory_space=pl.ANY)
    vmem = pl.BlockSpec(memory_space=pltpu.VMEM)
    tokens = (2 * IMGS, OUT_ROWS, D)
    half = (IMGS, OUT_ROWS, D)
    piece = (SMALL_ROWS, RELS_PAD)
    low = pltpu.VMEM((ROWS, D), BF16)
    return pl.pallas_call(
        train_kernel,
        out_shape=[
            jax.ShapeDtypeStruct(tokens, BF16), jax.ShapeDtypeStruct(tokens, BF16),
            jax.ShapeDtypeStruct((128, PACKED), BF16), jax.ShapeDtypeStruct(piece, F32),
        ],
        in_specs=[pl.BlockSpec(memory_space=pltpu.SMEM), vmem] + [anywhere] * 5 + [vmem] * 6,
        out_specs=[anywhere] * 3 + [vmem],
        scratch_shapes=[
            pltpu.VMEM((2 * D, PACKED), BF16),
            pltpu.VMEM((2, ROWS, D), BF16),
            pltpu.VMEM((2, KROWS, 3 * D), BF16),
            pltpu.VMEM((2, ROWS, D), BF16),
            pltpu.VMEM((2, ROWS, D), F32),
            pltpu.VMEM((2, ROWS, FF), BF16),
            pltpu.VMEM((2, ROWS, FF), BF16),
            pltpu.VMEM((2, 2, 2, 128, PACKED), BF16),
            pltpu.VMEM((2, 128, PACKED), BF16),
            land_shapes(0), land_shapes(1),
            tuple(pltpu.VMEM((3, 32, (hi - lo) // 4), BF16) for lo, hi, _ in STREAMS),
            pltpu.VMEM((128, PACKED), BF16),
            pltpu.VMEM((32, PAIR, KEYS), F32),
            pltpu.VMEM((2, 16, PAIR, KEYS), F32),
            low,
            pltpu.VMEM((D, ROWS), BF16),
            pltpu.VMEM((ROWS, D), F32),
            pltpu.VMEM((ROWS, 3 * D), BF16),
            low,
            low,
            pltpu.VMEM((IMGS, TOK, D), BF16),
            pltpu.VMEM((2,) + half, BF16),
            pltpu.VMEM(half, BF16),
            pltpu.VMEM((2,) + half, BF16),
            pltpu.VMEM(half, BF16),
            pltpu.VMEM((8, TINY_ROWS, RELS_PAD), F32),
            pltpu.VMEM((32, RELS_PAD), F32),
            pltpu.VMEM((2, 8, D), F32),
            pltpu.VMEM((2, 1, 3 * D), F32),
            pltpu.VMEM((2, 1, FF), F32),
            pltpu.VMEM((2, 8, D), F32),
            pltpu.VMEM((2, 1, FF), F32),
            pltpu.VMEM((2, 4) + piece, F32),
            pltpu.VMEM((4,) + piece, F32),
            pltpu.VMEM((3, 4) + piece, F32),
            pltpu.VMEM((3, 3) + piece, F32),
            pltpu.SemaphoreType.DMA((COPIES,)),
            pltpu.SemaphoreType.DMA((COPIES,)),
            pltpu.SemaphoreType.DMA((8,)),
            pltpu.SemaphoreType.REGULAR,
        ],
        compiler_params=pltpu.CompilerParams(
            collective_id=1, has_side_effects=True, vmem_limit_bytes=VMEM_LIMIT
        ),
        cost_estimate=pl.CostEstimate(
            flops=12 * ROWS * D * PACKED, bytes_accessed=16 << 20, transcendentals=6 * ROWS * FF
        ),
        name="train_layers",
    )(slots, images, cotangent, qkv, proj, up, down, tiny, places, mask, order, back, turn)


def block_pair(blocks, fill):
    lead = blocks.shape[:-3]
    none = [(0, 0)] * len(lead)
    pad_rows = [(0, WPAD - WTOK)]
    first = jnp.pad(blocks[..., 0, :, :], none + pad_rows + [(0, KEYS - WTOK)], constant_values=fill)
    second = jnp.pad(
        blocks[..., 1, :, :], none + pad_rows + [(WPAD, KEYS - WTOK - WPAD)], constant_values=fill
    )
    return jnp.concatenate([first, second], axis=-2)


def inside_blocks():
    rows, cols = np.arange(PAIR)[:, None] // WPAD, np.arange(KEYS)[None, :]
    return (cols // WPAD == rows) & (cols % WPAD < WTOK) & (cols < PAIR)


def on_device(
    images, cotangent, micro_order, region_ids, rel_index, qkv_weight, proj_weight, up_weight,
    down_weight, bias_table, norm_gains, offsets, hidden_bias,
):
    first_section = lax.axis_index("pipe") == 0
    table_rows = bias_table.shape[1]

    def lanes(block, rows):
        return jnp.pad(
            block.astype(F32), ((0, rows - block.shape[0]), (0, RELS_PAD - block.shape[1]))
        )

    tiny = jnp.concatenate(
        [
            lanes(jnp.concatenate([norm_gains[0], offsets[0]]), 8),
            lanes(hidden_bias[0].reshape(4, 128), 8),
            lanes(bias_table[0].T, 8),
        ]
    )
    places = jnp.pad(rel_index, ((0, WPAD - WTOK), (0, KEYS - WTOK)), constant_values=-1)
    regions = region_ids.reshape(2, WIN, 2, WIN).transpose(0, 2, 1, 3).reshape(2, 2, WTOK)
    regions = jnp.pad(regions, ((0, 0), (0, 0), (0, WPAD - WTOK))).reshape(2, PAIR)
    queries = regions[:, :, None]
    keys = jnp.pad(regions, ((0, 0), (0, KEYS - PAIR)))[:, None, :]
    inside = inside_blocks()
    mask0 = np.broadcast_to(np.where(inside, 0.0, BLOCKED), (2, PAIR, KEYS)).astype(np.float32)
    mask1 = jnp.where(inside[None], jnp.where(queries == keys, 0.0, -1e9), BLOCKED).astype(F32)
    mask = jnp.stack([jnp.asarray(mask0), mask1])
    order = jnp.asarray(np.stack([order_matrix(0), order_matrix(SHIFT)]), BF16)
    back = jnp.asarray(np.stack([back_matrix(0), back_matrix(SHIFT)]), BF16)
    turn = jnp.asarray(np.stack([turn_matrix(0, SHIFT), turn_matrix(SHIFT, 0)]), BF16)
    slot_order = micro_order[0]

    layer_out, dx_slots, share, sums = train(
        slot_order, images, cotangent, qkv_weight, proj_weight, up_weight, down_weight, tiny, places,
        mask, order, back, turn,
    )
    slots = jnp.arange(2 * IMGS, dtype=jnp.int32)
    inverse = jnp.sum(jnp.where(slot_order[:, None] == slots[None, :], slots[:, None], 0), axis=0)
    picks = jnp.where(first_section, inverse, slots)
    input_grad = jnp.take(dx_slots[:, :TOK], picks, axis=0).astype(F32)
    down = jnp.concatenate(
        [share[:, DOWN0 + k * D : DOWN0 + (k + 1) * D] for k in range(4)], axis=0
    )
    return (
        layer_out[None, :, :TOK],
        input_grad[None],
        share[None, :, QKV0:PROJ0].astype(F32),
        share[None, :, PROJ0:UP0].astype(F32),
        share[None, :, UP0:DOWN0].astype(F32),
        down[None].astype(F32),
        sums[16:20, :table_rows].T[None],
        sums[None, 0:2, 0:128],
        sums[None, 2:8, 0:128],
        sums[8:12, 0:128].reshape(1, D),
    )


def solution(mesh):
    rows = P(("shard", "rep"), None, None)
    split = P("pipe", "shard", None)
    lanes = P("pipe", None, "shard")
    return jax.shard_map(
        on_device,
        mesh=mesh,
        in_specs=(
            rows, rows, P(("shard", "rep"), None), P(), P(),
            split, split, split, split, lanes, lanes, lanes, P("pipe", "shard"),
        ),
        out_specs=(
            P("pipe", ("shard", "rep"), None, None), P("pipe", ("shard", "rep"), None, None),
            split, split, split, split, lanes, lanes, lanes, P("pipe", "shard"),
        ),
        check_vma=False,
    )
```

time: 622 us -> 191 us (0.31)
  waiting for transfers between devices: 450 us -> 0 us
  Pallas kernels: 91.9 us -> 169 us
  other arithmetic: 21.4 us -> 5.63 us
  blocking collectives: 14.2 us -> 0 us
  between operations: 14.4 us -> 0.85 us
  local copies, waits for them, and re-layouts: 22.8 us -> 14.7 us
    psum x2 -> x0, waiting for transfers between devices: 221 us -> none  [the longest x1 139 us: on_device(): flat = lax.psum(flat, everyone)]
    reduce_scatter x1 -> x0, waiting for transfers between devices: 125 us -> none  [reduce_big(): lax.psum_scatter(big, ('pipe', 'shard'), scatter_dimension=0, tiled=True)]
    all_gather x1 -> x0, waiting for transfers between devices: 103 us -> none  [on_device(): packed = lax.all_gather(mine, both, axis=0, tiled=True)]
    pallas_call x4 -> x1, Pallas kernels: 91.9 us -> 169 us  [train(): pl.pallas_call(train_kernel, out_shape=[jax.ShapeDtypeStruct(tokens, BF16...]
    all_gather x1 -> x0, blocking collectives: 14.2 us -> none  [on_device(): tiny = lax.all_gather(tiny, both, axis=0).reshape(2, shards, 32, 128)]
    concatenate x6 -> x2, other arithmetic: 12.6 us -> 0.62 us  [the longest x1 0.61 us: on_device(): jnp.concatenate([lanes(jnp.concatenate([norm_gains[0], offsets[0]]), 8),...]
  transfers between devices with their start and end apart: 6 -> 0, of which waited for: 4 -> 0; matrix products, arithmetic and copies ran while one was open for 5% -> 0% of each run, Pallas kernels for 0% -> 0%
where the time goes in v2:
time: 191 us
  Pallas kernels  169 us (88%)
  local copies, waits for them, and re-layouts  14.7 us (8%)
  other arithmetic  5.63 us (3%)
    pallas_call x1, Pallas kernels, train(): pl.pallas_call(train_kernel, out_shape=[jax.ShapeDtypeStruct(tokens, BF16...  169 us
    unnamed x29, local copies, waits for them, and re-layouts  7.4 us

profile of v2, /device:TPU:0, one launch (start us, length us, event | category | flops | bytes accessed | tf_op | source)
XLA Modules:
  0.0 190.6 jit_solution(10002555257961929347)
XLA Ops:
  0.7 0.0 copy-start.5
  0.7 0.0 copy-start.3
  0.7 2.2 %copy.40.images_ref = bf16[4,196,512]{2,1,0:T(8,128)(2,1)} copy(bf16[4,196,512]{2,0,1:T(4,128)(2,1)} %param.18) | data formatting | bytes 1605632 | tf_op args[0]
  3.0 1.0 copy.41.cot_hbm
  4.0 0.0 copy-done.8
  4.1 0.6 fusion.6.tiny_ref
  4.7 0.0 copy-done.4
  4.7 0.6 pad.30.places_ref
  5.3 0.1 reshape.144
  5.4 0.1 reshape.145
  5.5 0.1 eq.38
  5.6 0.1 select_select_fusion
  5.7 0.7 pad_maximum_fusion.mask_ref
  6.5 169.4 %train_layers.1 = (bf16[4,208,512]{2,1,0:T(8,128)(2,1)}, bf16[4,208,512]{2,1,0:T(8,128)(2,1)}, bf16[128,6144]{1,0:T(8,128)(2,1)}, f32[24,256]{1,0:T(8,128)}) custom-call(s32[4]{0:T(128)} %bitcast.52, bf16[4,196,512]{2,1,0:T(8,128)(2,1)} %copy.40.images_ref, bf16[4,196,512]{2,1,0:T(8,128)(2,1)} %copy.41.cot_hbm, bf16[1,128,1536]{2,1,0:T(8,128)(2,1)} %qkv_hbm.1, ...), custom_call_target="tpu_custom_call" | custom-call | flops 16911433728 | bytes 16777216 | tf_op jit(solution)/shard_map/train_layers/pallas_call | solution.py:759
  175.9 1.3 slice_bitcast_fusion
  177.1 0.0 copy-start.11
  177.2 1.3 copy.42
  178.5 0.0 copy-done.2
  178.5 0.1 slice.40
  178.5 0.1 select_reduce_fusion
  178.6 0.6 gather_fusion
  179.3 0.2 fusion
  179.4 2.2 %copy.43 = f32[1,4,196,512]{3,1,2,0:T(4,128)} copy(f32[1,4,196,512]{3,2,1,0:T(8,128)S(1)} %fusion) | data formatting | bytes 3211264
  181.6 1.0 bitcast_convert_fusion.1
  182.6 0.8 slice_bitcast_fusion.4
  183.4 1.1 bitcast_convert_fusion
  184.4 1.1 maximum_convert_fusion
  185.5 1.3 slice_bitcast_fusion.6
  186.8 1.2 slice_bitcast_fusion.7
  188.1 0.7 slice_bitcast_fusion.5
  188.7 0.6 copy.44
  189.3 1.3 slice.51
  (26 shorter events, 0.1 us)
Async XLA Ops:
  0.6 2.3 %copy-start.1 = (bf16[4,196,512]{2,0,1:T(4,128)(2,1)S(1)}, bf16[4,196,512]{2,0,1:T(4,128)(2,1)}, u32[]{:S(2)}) copy-start(bf16[4,196,512]{2,0,1:T(4,128)(2,1)} %param.19) | copy-start | bytes 2408452
  0.7 3.4 %copy-start.7 = (bf16[1,512]{1,0:T(2,128)(2,1)S(1)}, bf16[1,512]{1,0:T(2,128)(2,1)}, u32[]{:S(2)}) copy-start(bf16[1,512]{1,0:T(2,128)(2,1)} %param.30) | copy-start | bytes 3076
  0.7 3.4 %copy-start.8 = (bf16[1,6,128]{2,1,0:T(8,128)(2,1)S(1)}, bf16[1,6,128]{2,1,0:T(8,128)(2,1)}, u32[]{:S(2)}) copy-start(bf16[1,6,128]{2,1,0:T(8,128)(2,1)} %param.29) | copy-start | bytes 4612
  0.7 3.4 %copy-start.10 = (bf16[1,2,128]{2,1,0:T(2,128)(2,1)S(1)}, bf16[1,2,128]{2,1,0:T(2,128)(2,1)}, u32[]{:S(2)}) copy-start(bf16[1,2,128]{2,1,0:T(2,128)(2,1)} %param.28) | copy-start | bytes 1540
  0.7 3.4 %copy-start.6 = (bf16[1,169,4]{1,2,0:T(4,128)(2,1)S(1)}, bf16[1,169,4]{1,2,0:T(4,128)(2,1)}, u32[]{:S(2)}) copy-start(bf16[1,169,4]{1,2,0:T(4,128)(2,1)} %param.27) | copy-start | bytes 4060
  0.7 4.0 %copy-start.4 = (s32[49,49]{1,0:T(8,128)S(1)}, s32[49,49]{1,0:T(8,128)}, u32[]{:S(2)}) copy-start(s32[49,49]{1,0:T(8,128)} %param.22) | copy-start | bytes 28816
  0.7 4.6 %copy-start.9 = (s32[196]{0:T(256)S(1)}, s32[196]{0:T(256)}, u32[]{:S(2)}) copy-start(s32[196]{0:T(256)} %param.21) | copy-start | bytes 2356
  0.7 4.9 %copy-start.5 = (pred[112,128]{1,0:T(8,128)(4,1)S(1)}, pred[112,128]{1,0:T(8,128)(4,1)}, u32[]{:S(2)}) copy-start(pred[112,128]{1,0:T(8,128)(4,1)} %constant.73) | copy-start | bytes 43012
  0.7 5.0 %copy-start.3 = (f32[1,2,112,128]{3,2,1,0:T(8,128)S(1)}, f32[1,2,112,128]{3,2,1,0:T(8,128)}, u32[]{:S(2)}) copy-start(f32[1,2,112,128]{3,2,1,0:T(8,128)} %constant.72) | copy-start | bytes 344068
  175.9 2.6 %copy-start.2 = (bf16[4,208,512]{2,1,0:T(8,128)(2,1)S(1)}, bf16[4,208,512]{2,1,0:T(8,128)(2,1)}, u32[]{:S(2)}) copy-start(bf16[4,208,512]{2,1,0:T(8,128)(2,1)} %get-tuple-element.15) | copy-start | bytes 2555908
  177.1 1.4 copy-start.11
  179.4 2.2 %copy-start = (bf16[128,6144]{1,0:T(8,128)(2,1)S(1)}, bf16[128,6144]{1,0:T(8,128)(2,1)}, u32[]{:S(2)}) copy-start(bf16[128,6144]{1,0:T(8,128)(2,1)} %get-tuple-element.16) | copy-start | bytes 4718596

commit v3 on v2

--- a/solution.py
+++ b/solution.py
@@ -110,7 +110,7 @@
 
 
 MESH = pl.DeviceIdType.MESH
-STREAMS = ((2048, 4096, "xz"), (4096, 6144, "zx"), (0, 1024, "xz"), (1024, 2048, "zx"))
+STREAMS = ((1536, 4096, "xz"), (4096, 6144, "zx"), (0, 512, "xz"), (512, 1536, "zx"))
 LATE = (2, 3)
 TINY_ROWS = 24
 SMALL_ROWS = 24
@@ -168,7 +168,9 @@
     pass
 
 
-def forward_body(params, saved, x_ref, low_ref, acc_ref, after_attend=nothing):
+def forward_body(
+    params, saved, x_ref, low_ref, acc_ref, after_qkv=nothing, after_attend=nothing, before_mlp=nothing
+):
     w_ref, small_ref, qbias_ref, hbias_ref, rel_ref, mask_ref = params
     qkv_ref, o_ref, r_ref, act_ref, slope_ref = saved
     n1, _ = normalised(x_ref[...].astype(F32))
@@ -182,6 +184,7 @@
         return 0
 
     lax.fori_loop(0, 3 * D // CHUNK, qkv_step, 0)
+    after_qkv()
     masks = head_masks(PAIR)
 
     def attend(i, _):
@@ -206,6 +209,7 @@
     n2, _ = normalised(r)
     low_ref[...] = (n2 * small_ref[1:2] + small_ref[3:4]).astype(BF16)
     acc_ref[...] = r + small_ref[7:8]
+    before_mlp()
 
     def mlp(c, _):
         cols = pl.ds(pl.multiple_of(c * CHUNK, CHUNK), CHUNK)
@@ -225,7 +229,8 @@
 
 def backward_body(
     params, saved, x_ref, dy_ref, results, scratch,
-    in_mlp=nothing, after_mlp=nothing, before_attend=nothing, after_attend=nothing, after_weights=nothing,
+    in_mlp=nothing, after_mlp=nothing, after_proj=nothing, before_attend=nothing, after_attend=nothing,
+    after_weights=nothing,
 ):
     w_ref, small_ref, _, _, rel_ref, mask_ref = params
     qkv_ref, o_ref, r_ref, act_ref, slope_ref = saved
@@ -281,6 +286,9 @@
             slice(PROJ0 + n * CHUNK, PROJ0 + (n + 1) * CHUNK),
             dot(turned_ref[...], low_ref[:, cols]).astype(BF16),
         )
+    after_proj()
+    for n in range(D // CHUNK):
+        cols = slice(n * CHUNK, (n + 1) * CHUNK)
         rows_of = w_ref[n * CHUNK : (n + 1) * CHUNK, PROJ0 : PROJ0 + D]
         do_ref[:, cols] = dot(low_ref[...], rows_of, ((1,), (1,))).astype(BF16)
     before_attend()
@@ -369,7 +377,7 @@
     return total[0:16] + total[16:32]
 
 
-COPIES = 192
+COPIES = 224
 
 
 def piece_of(region):
@@ -421,35 +429,74 @@
     for local in locals_in:
         local.wait()
 
-    width = PACKED // 8
-
-    def quarter(half, part, index):
-        return (half * 64, 64), (pl.multiple_of(part * (PACKED // 2) + index * width, 128), width)
-
-    def weight_piece(y, region):
-        (r0, nr), cols = region
-        start = pl.multiple_of(block_index(y, me["core"]) * 128 + r0, 64)
-        return w_ref.at[pl.ds(start, nr), pl.ds(*cols)]
-
-    first_base = copies.count
-    for half in range(2):
+    span = PACKED // 3
+    width = span // 8
+
+    def weight_piece(y, lo, size):
+        start = pl.multiple_of(block_index(y, me["core"]) * 128, 128)
+        return w_ref.at[pl.ds(start, 128), pl.ds(lo, size)]
+
+    def quarter(chunk, part, index):
+        return pl.multiple_of(chunk * span + part * (span // 2) + index * width, 128), width
+
+    first_base = {}
+
+    def set_off(chunk):
+        first_base[chunk] = copies.count
         for k in (1, 2, 3):
             for part, axis in enumerate("xz"):
-                piece = weight_piece(me["y"], quarter(half, part, me[axis]))
+                piece = weight_piece(me["y"], *quarter(chunk, part, me[axis]))
                 copies.start(piece, piece, moved(me, "y", k))
-    own_block = w_ref.at[own_rows]
-    to_partner = {"own": copies.start(own_block, own_block, partner)}
+
+    to_partner = {}
+    set_off(0)
     tiny_copies = [
         copies.start(tiny_ref, tiny_land.at[own], place) for place in [partner] + peers["y"] + across
     ]
+    for chunk in range(3):
+        piece = weight_piece(me["y"], chunk * span, span)
+        to_partner["own", chunk] = copies.start(piece, piece, partner)
     tiny_land[own] = tiny_ref[...]
 
     for b in range(IMGS):
         picture = images_ref[slots_ref[pipe * IMGS + b]]
         x_ref[0, b * IMG_ROWS : (b + 1) * IMG_ROWS] = dot(order_ref[0], picture).astype(BF16)
+    set_off(1)
     cot_copy.wait()
     for b in range(IMGS):
         dy_ref[b * IMG_ROWS : (b + 1) * IMG_ROWS] = dot(order_ref[1], cot_ref[b]).astype(BF16)
+
+    steps = [2 - pipe, 1 + 2 * pipe, 3 - pipe]
+    seconds = {}
+
+    def pass_on(chunk, slots):
+        for slot in slots:
+            y = (me["y"] - steps[slot] + 4) % 4
+            for part, axis in enumerate("xz"):
+                piece = weight_piece(y, *quarter(chunk, part, me[axis]))
+                index = first_base[chunk] + (steps[slot] - 1) * 2 + part
+                pltpu.make_async_remote_copy(
+                    src_ref=piece, dst_ref=piece, send_sem=send_sem.at[index],
+                    recv_sem=recv_sem.at[index], device_id=device_at(partner), device_id_type=MESH,
+                ).wait_recv()
+                for j in (1, 3, 2):
+                    seconds[chunk, slot, part, j] = copies.start(piece, piece, moved(me, axis, j))
+
+    def hand_over(chunk, slots):
+        for slot in slots:
+            y = (me["y"] - steps[slot] + 4) % 4
+            for part in range(2):
+                for j in (1, 3, 2):
+                    seconds[chunk, slot, part, j].wait_recv()
+            piece = weight_piece(y, chunk * span, span)
+            to_partner[slot, chunk] = copies.start(piece, piece, partner)
+
+    def arrived(chunk, slots):
+        for slot in slots:
+            to_partner[slot, chunk].wait_recv()
+
+    pass_on(0, (0, 1))
+    set_off(2)
     for copy in tiny_copies:
         copy.wait_recv()
     qbias_ref[...] = jnp.zeros_like(qbias_ref)
@@ -464,42 +511,10 @@
                 tables_ref[head : head + 1] = rows[16 + j : 17 + j]
         qbias_ref[layer, :, 0:D] = small_ref[layer, 4:5]
         qbias_ref[layer, :, 2 * D : 3 * D] = small_ref[layer, 5:6]
-
-    steps = [2 - pipe, 1 + 2 * pipe, 3 - pipe]
-    seconds = {}
-
-    def pass_on(slot):
-        y = (me["y"] - steps[slot] + 4) % 4
-        for half in range(2):
-            for part, axis in enumerate("xz"):
-                piece = weight_piece(y, quarter(half, part, me[axis]))
-                index = first_base + half * 6 + (steps[slot] - 1) * 2 + part
-                pltpu.make_async_remote_copy(
-                    src_ref=piece, dst_ref=piece, send_sem=send_sem.at[index],
-                    recv_sem=recv_sem.at[index], device_id=device_at(partner), device_id_type=MESH,
-                ).wait_recv()
-                for j in (1, 3, 2):
-                    seconds[slot, half, part, j] = copies.start(piece, piece, moved(me, axis, j))
-
-    def hand_over(slot):
-        y = (me["y"] - steps[slot] + 4) % 4
-        for half in range(2):
-            for part in range(2):
-                for j in (1, 3, 2):
-                    seconds[slot, half, part, j].wait_recv()
-            piece = weight_piece(y, ((half * 64, 64), (0, PACKED)))
-            to_partner[slot, half] = copies.start(piece, piece, partner)
-
-    pass_on(0)
-    pass_on(1)
     table_rows_of(tables_ref, places_ref, rel_ref)
-    hand_over(0)
-    hand_over(1)
-    pass_on(2)
-    to_partner["own"].wait_recv()
-    for slot in range(2):
-        for half in range(2):
-            to_partner[slot, half].wait_recv()
+    hand_over(0, (0, 1))
+    pass_on(1, (0, 1))
+    arrived(0, ("own", 0, 1))
 
     def params(layer):
         return (
@@ -517,11 +532,31 @@
             if turned is not None:
                 turned[b * IMG_ROWS : (b + 1) * IMG_ROWS] = dot(turn_ref[layer], own_rows).astype(BF16)
 
-    y0 = forward_body(params(0), saved(0), x_ref.at[0], low_ref, du_ref, lambda: hand_over(2))
+    def before_mlp0():
+        hand_over(2, (0, 1))
+        for chunk in range(3):
+            pass_on(chunk, (2,))
+        arrived(1, ("own", 0, 1))
+        arrived(2, ("own", 0, 1))
+
+    def after_qkv1():
+        hand_over(1, (2,))
+        hand_over(2, (2,))
+
+    def before_mlp1():
+        arrived(1, (2,))
+        arrived(2, (2,))
+
+    y0 = forward_body(
+        params(0), saved(0), x_ref.at[0], low_ref, du_ref, after_qkv=lambda: pass_on(2, (0, 1)),
+        after_attend=lambda: hand_over(1, (0, 1)), before_mlp=before_mlp0,
+    )
+    hand_over(0, (2,))
     in_token_order(0, y0, y_ref.at[0], x_ref.at[1])
-    for half in range(2):
-        to_partner[2, half].wait_recv()
-    y1 = forward_body(params(1), saved(1), x_ref.at[1], low_ref, du_ref)
+    arrived(0, (2,))
+    y1 = forward_body(
+        params(1), saved(1), x_ref.at[1], low_ref, du_ref, after_qkv=after_qkv1, before_mlp=before_mlp1
+    )
     in_token_order(1, y1, y_ref.at[1], None)
     neighbour = {**me, "y": me["y"] + 1 - 2 * pipe}
     y_copy = copies.start(y_ref.at[1 - pipe], y_land, neighbour)
@@ -633,13 +668,14 @@
     scratch = (low_ref, turned_ref, du_ref, dqkv_ref, do_ref)
 
     def before_attend1():
-        add_core(1, early)
-        send(1, early, 0)
+        for t in (1, 0):
+            add_core(1, (t,))
+            send(1, (t,), 0)
 
     dx1 = backward_body(
         params(1), saved(1), x_ref.at[1], dy_ref, results(1), scratch,
-        after_mlp=lambda: send_core(1, early), before_attend=before_attend1,
-        after_weights=lambda: send_core(1, late),
+        after_mlp=lambda: send_core(1, (1,)), after_proj=lambda: send_core(1, (0,)),
+        before_attend=before_attend1, after_weights=lambda: send_core(1, late),
     )
     in_token_order(1, dx1, dx_ref.at[1], dy_ref)
     add_core(1, late)
@@ -647,27 +683,33 @@
     send(1, late, 0)
 
     def in_mlp0():
-        add(1, early, 0)
-        send(1, early, 1)
+        add(1, (1, 0), 0)
+        send(1, (1, 0), 1)
 
     def after_mlp0():
         pl.semaphore_wait(free_sem, 1)
-        send_core(0, early)
+        send_core(0, (1,))
         add(1, late, 0)
         send(1, late, 1)
 
     def before_attend0():
-        add_core(0, early)
-        send(0, early, 0)
+        for t in (1, 0):
+            add_core(0, (t,))
+            send(0, (t,), 0)
+
+    def after_attend0():
+        add(1, early, 1)
+        add(1, late, 1)
 
     def after_weights0():
         send_core(0, late)
-        add(1, early, 1)
-        add(1, late, 1)
+        add(0, (1,), 0)
+        send(0, (1,), 1)
 
     dx0 = backward_body(
         params(0), saved(0), x_ref.at[0], dy_ref, results(0), scratch,
-        in_mlp=in_mlp0, after_mlp=after_mlp0, before_attend=before_attend0, after_weights=after_weights0,
+        in_mlp=in_mlp0, after_mlp=after_mlp0, after_proj=lambda: send_core(0, (0,)),
+        before_attend=before_attend0, after_attend=after_attend0, after_weights=after_weights0,
     )
     add_core(0, late)
     send(0, late, 0)
@@ -675,8 +717,8 @@
     dx_copy = copies.start(dx_ref.at[1 - pipe], dx_land, neighbour)
     dx_keep = pltpu.make_async_copy(dx_ref.at[pipe], dx_hbm.at[pl.ds(pipe * IMGS, IMGS)], local_sem.at[1])
     dx_keep.start()
-    add(0, early, 0)
-    send(0, early, 1)
+    add(0, (0,), 0)
+    send(0, (0,), 1)
 
     for layer in range(2):
         gtable = table_sums(gbias_ref.at[layer], places_ref)

time: 191 us -> 174 us (0.911)
  Pallas kernels: 169 us -> 153 us
    pallas_call x1, Pallas kernels: 169 us -> 153 us  [train(): pl.pallas_call(train_kernel, out_shape=[jax.ShapeDtypeStruct(tokens, BF16...]
where the time goes in v3:
time: 174 us
  Pallas kernels  153 us (88%)
  local copies, waits for them, and re-layouts  14.7 us (8%)
  other arithmetic  5.63 us (3%)
    pallas_call x1, Pallas kernels, train(): pl.pallas_call(train_kernel, out_shape=[jax.ShapeDtypeStruct(tokens, BF16...  153 us
    unnamed x29, local copies, waits for them, and re-layouts  7.4 us

profile of v3, /device:TPU:0, one launch (start us, length us, event | category | flops | bytes accessed | tf_op | source)
XLA Modules:
  0.0 173.9 jit_solution(16467500815332693528)
XLA Ops:
  0.6 0.0 copy-start.1
  0.7 0.0 copy-start.7
  0.7 0.0 copy-start.8
  0.7 0.0 copy-start.5
  0.7 0.0 copy-start.3
  0.7 2.2 %copy.40.images_ref = bf16[4,196,512]{2,1,0:T(8,128)(2,1)} copy(bf16[4,196,512]{2,0,1:T(4,128)(2,1)} %param.18) | data formatting | bytes 1605632 | tf_op args[0]
  3.0 1.0 copy.41.cot_hbm
  4.1 0.6 fusion.6.tiny_ref
  4.7 0.6 pad.30.places_ref
  5.3 0.1 reshape.144
  5.4 0.1 reshape.145
  5.5 0.1 eq.38
  5.6 0.1 select_select_fusion
  5.7 0.7 pad_maximum_fusion.mask_ref
  6.5 152.7 %train_layers.1 = (bf16[4,208,512]{2,1,0:T(8,128)(2,1)}, bf16[4,208,512]{2,1,0:T(8,128)(2,1)}, bf16[128,6144]{1,0:T(8,128)(2,1)}, f32[24,256]{1,0:T(8,128)}) custom-call(s32[4]{0:T(128)} %bitcast.52, bf16[4,196,512]{2,1,0:T(8,128)(2,1)} %copy.40.images_ref, bf16[4,196,512]{2,1,0:T(8,128)(2,1)} %copy.41.cot_hbm, bf16[1,128,1536]{2,1,0:T(8,128)(2,1)} %qkv_hbm.1, ...), custom_call_target="tpu_custom_call" | custom-call | flops 16911433728 | bytes 16777216 | tf_op jit(solution)/shard_map/train_layers/pallas_call | solution.py:801
  159.1 1.3 slice_bitcast_fusion
  160.4 0.0 copy-start.11
  160.4 1.3 copy.42
  161.7 0.1 slice.40
  161.8 0.1 select_reduce_fusion
  161.9 0.6 gather_fusion
  162.5 0.2 fusion
  162.7 2.2 %copy.43 = f32[1,4,196,512]{3,1,2,0:T(4,128)} copy(f32[1,4,196,512]{3,2,1,0:T(8,128)S(1)} %fusion) | data formatting | bytes 3211264
  164.9 1.0 bitcast_convert_fusion.1
  165.9 0.8 slice_bitcast_fusion.4
  166.6 1.1 bitcast_convert_fusion
  167.7 1.1 maximum_convert_fusion
  168.8 1.3 slice_bitcast_fusion.6
  170.1 1.2 slice_bitcast_fusion.7
  171.3 0.7 slice_bitcast_fusion.5
  172.0 0.6 copy.44
  172.6 1.3 slice.51
  (26 shorter events, 0.1 us)
Async XLA Ops:
  0.6 2.3 %copy-start.1 = (bf16[4,196,512]{2,0,1:T(4,128)(2,1)S(1)}, bf16[4,196,512]{2,0,1:T(4,128)(2,1)}, u32[]{:S(2)}) copy-start(bf16[4,196,512]{2,0,1:T(4,128)(2,1)} %param.19) | copy-start | bytes 2408452
  0.7 3.4 %copy-start.7 = (bf16[1,512]{1,0:T(2,128)(2,1)S(1)}, bf16[1,512]{1,0:T(2,128)(2,1)}, u32[]{:S(2)}) copy-start(bf16[1,512]{1,0:T(2,128)(2,1)} %param.30) | copy-start | bytes 3076
  0.7 3.4 %copy-start.8 = (bf16[1,6,128]{2,1,0:T(8,128)(2,1)S(1)}, bf16[1,6,128]{2,1,0:T(8,128)(2,1)}, u32[]{:S(2)}) copy-start(bf16[1,6,128]{2,1,0:T(8,128)(2,1)} %param.29) | copy-start | bytes 4612
  0.7 3.4 %copy-start.10 = (bf16[1,2,128]{2,1,0:T(2,128)(2,1)S(1)}, bf16[1,2,128]{2,1,0:T(2,128)(2,1)}, u32[]{:S(2)}) copy-start(bf16[1,2,128]{2,1,0:T(2,128)(2,1)} %param.28) | copy-start | bytes 1540
  0.7 3.4 %copy-start.6 = (bf16[1,169,4]{1,2,0:T(4,128)(2,1)S(1)}, bf16[1,169,4]{1,2,0:T(4,128)(2,1)}, u32[]{:S(2)}) copy-start(bf16[1,169,4]{1,2,0:T(4,128)(2,1)} %param.27) | copy-start | bytes 4060
  0.7 4.0 %copy-start.4 = (s32[49,49]{1,0:T(8,128)S(1)}, s32[49,49]{1,0:T(8,128)}, u32[]{:S(2)}) copy-start(s32[49,49]{1,0:T(8,128)} %param.22) | copy-start | bytes 28816
  0.7 4.6 %copy-start.9 = (s32[196]{0:T(256)S(1)}, s32[196]{0:T(256)}, u32[]{:S(2)}) copy-start(s32[196]{0:T(256)} %param.21) | copy-start | bytes 2356
  0.7 4.9 %copy-start.5 = (pred[112,128]{1,0:T(8,128)(4,1)S(1)}, pred[112,128]{1,0:T(8,128)(4,1)}, u32[]{:S(2)}) copy-start(pred[112,128]{1,0:T(8,128)(4,1)} %constant.73) | copy-start | bytes 43012
  0.7 5.0 %copy-start.3 = (f32[1,2,112,128]{3,2,1,0:T(8,128)S(1)}, f32[1,2,112,128]{3,2,1,0:T(8,128)}, u32[]{:S(2)}) copy-start(f32[1,2,112,128]{3,2,1,0:T(8,128)} %constant.72) | copy-start | bytes 344068
  159.1 2.6 %copy-start.2 = (bf16[4,208,512]{2,1,0:T(8,128)(2,1)S(1)}, bf16[4,208,512]{2,1,0:T(8,128)(2,1)}, u32[]{:S(2)}) copy-start(bf16[4,208,512]{2,1,0:T(8,128)(2,1)} %get-tuple-element.15) | copy-start | bytes 2555908
  160.4 1.4 copy-start.11
  162.7 2.2 %copy-start = (bf16[128,6144]{1,0:T(8,128)(2,1)S(1)}, bf16[128,6144]{1,0:T(8,128)(2,1)}, u32[]{:S(2)}) copy-start(bf16[128,6144]{1,0:T(8,128)(2,1)} %get-tuple-element.16) | copy-start | bytes 4718596

commit v4 on v3

--- a/solution.py
+++ b/solution.py
@@ -98,7 +98,7 @@
     bias = rel_ref[pl.ds(g * 4, 4)].astype(F32) + mask_ref[lax.rem(i, 2)][None]
     s = s + bias.reshape(4 * PAIR, KEYS)
     e = jnp.exp(s - jnp.max(s, -1, keepdims=True))
-    return e / jnp.sum(e, -1, keepdims=True)
+    return e * (1.0 / jnp.sum(e, -1, keepdims=True))
 
 
 def down_chunk(w_ref, c):
@@ -157,10 +157,11 @@
             copy.wait_send()
 
 
-def greet(places):
+def greet(places, meanwhile):
     barrier = pltpu.get_barrier_semaphore()
     for place in places:
         pl.semaphore_signal(barrier, inc=1, device_id=device_at(place), device_id_type=MESH)
+    meanwhile()
     pl.semaphore_wait(barrier, len(places))
 
 
@@ -358,8 +359,8 @@
 
 
 def table_sums(gbias_ref, places_ref):
-    second = gbias_ref[:, WPAD:PAIR].reshape(16 * WPAD, KEYS)
-    gbias_ref[:, 0:WPAD] += pltpu.roll(second, KEYS - WPAD, 1).reshape(16, WPAD, KEYS)
+    second = gbias_ref[:, WPAD:PAIR].reshape(32 * WPAD, KEYS)
+    gbias_ref[:, 0:WPAD] += pltpu.roll(second, KEYS - WPAD, 1).reshape(32, WPAD, KEYS)
     entry = lax.broadcasted_iota(jnp.int32, (RELS_PAD, KEYS), 0)
 
     def rows(n, total):
@@ -373,8 +374,8 @@
             parts.append(dot(jnp.concatenate([high, low], axis=0), hot, ((1,), (1,))))
         return total + sum(parts)
 
-    total = lax.fori_loop(0, WIN, rows, jnp.zeros((32, RELS_PAD), F32))
-    return total[0:16] + total[16:32]
+    total = lax.fori_loop(0, WIN, rows, jnp.zeros((64, RELS_PAD), F32))
+    return total[0:32] + total[32:64]
 
 
 COPIES = 224
@@ -425,9 +426,18 @@
         locals_in.append(local)
     cot_copy = pltpu.make_async_copy(cot_hbm.at[pl.ds(pipe * IMGS, IMGS)], cot_ref, local_sem.at[7])
     cot_copy.start()
-    greet([partner] + across + [place for axis in "yxz" for place in peers[axis]])
-    for local in locals_in:
-        local.wait()
+
+    def order_tokens():
+        for b in range(IMGS):
+            picture = images_ref[slots_ref[pipe * IMGS + b]]
+            x_ref[0, b * IMG_ROWS : (b + 1) * IMG_ROWS] = dot(order_ref[0], picture).astype(BF16)
+        cot_copy.wait()
+        for b in range(IMGS):
+            dy_ref[b * IMG_ROWS : (b + 1) * IMG_ROWS] = dot(order_ref[1], cot_ref[b]).astype(BF16)
+        for local in locals_in:
+            local.wait()
+
+    greet([partner] + across + [place for axis in "yxz" for place in peers[axis]], order_tokens)
 
     span = PACKED // 3
     width = span // 8
@@ -457,14 +467,6 @@
         piece = weight_piece(me["y"], chunk * span, span)
         to_partner["own", chunk] = copies.start(piece, piece, partner)
     tiny_land[own] = tiny_ref[...]
-
-    for b in range(IMGS):
-        picture = images_ref[slots_ref[pipe * IMGS + b]]
-        x_ref[0, b * IMG_ROWS : (b + 1) * IMG_ROWS] = dot(order_ref[0], picture).astype(BF16)
-    set_off(1)
-    cot_copy.wait()
-    for b in range(IMGS):
-        dy_ref[b * IMG_ROWS : (b + 1) * IMG_ROWS] = dot(order_ref[1], cot_ref[b]).astype(BF16)
 
     steps = [2 - pipe, 1 + 2 * pipe, 3 - pipe]
     seconds = {}
@@ -495,6 +497,7 @@
         for slot in slots:
             to_partner[slot, chunk].wait_recv()
 
+    set_off(1)
     pass_on(0, (0, 1))
     set_off(2)
     for copy in tiny_copies:
@@ -512,8 +515,9 @@
         qbias_ref[layer, :, 0:D] = small_ref[layer, 4:5]
         qbias_ref[layer, :, 2 * D : 3 * D] = small_ref[layer, 5:6]
     table_rows_of(tables_ref, places_ref, rel_ref)
+    pass_on(1, (0, 1))
     hand_over(0, (0, 1))
-    pass_on(1, (0, 1))
+    pass_on(2, (0, 1))
     arrived(0, ("own", 0, 1))
 
     def params(layer):
@@ -532,10 +536,12 @@
             if turned is not None:
                 turned[b * IMG_ROWS : (b + 1) * IMG_ROWS] = dot(turn_ref[layer], own_rows).astype(BF16)
 
-    def before_mlp0():
+    def after_attend0():
         hand_over(2, (0, 1))
         for chunk in range(3):
             pass_on(chunk, (2,))
+
+    def before_mlp0():
         arrived(1, ("own", 0, 1))
         arrived(2, ("own", 0, 1))
 
@@ -548,8 +554,8 @@
         arrived(2, (2,))
 
     y0 = forward_body(
-        params(0), saved(0), x_ref.at[0], low_ref, du_ref, after_qkv=lambda: pass_on(2, (0, 1)),
-        after_attend=lambda: hand_over(1, (0, 1)), before_mlp=before_mlp0,
+        params(0), saved(0), x_ref.at[0], low_ref, du_ref, after_qkv=lambda: hand_over(1, (0, 1)),
+        after_attend=after_attend0, before_mlp=before_mlp0,
     )
     hand_over(0, (2,))
     in_token_order(0, y0, y_ref.at[0], x_ref.at[1])
@@ -565,17 +571,18 @@
 
     core_copies, sent, regions = {}, {}, {}
 
-    def send_core(layer, streams):
+    def send_core(layer, streams, begin=0, end=PACKED):
         for t in streams:
-            lo, hi, _ = STREAMS[t]
-            core_copies[layer, t] = copies.start(
-                g_ref.at[layer, :, 1 - me["core"], :, lo:hi], core_ref.at[:, :, lo:hi], partner
+            lo, hi = max(STREAMS[t][0], begin), min(STREAMS[t][1], end)
+            core_copies.setdefault((layer, t), []).append(
+                copies.start(g_ref.at[layer, :, 1 - me["core"], :, lo:hi], core_ref.at[:, :, lo:hi], partner)
             )
 
     def add_core(layer, streams):
         for t in streams:
             lo, hi, _ = STREAMS[t]
-            core_copies[layer, t].wait_recv()
+            for copy in core_copies[layer, t]:
+                copy.wait_recv()
 
             def one(n, _, lo=lo, hi=hi):
                 half, rows = n // 4, pl.ds(pl.multiple_of((n % 4) * 32, 32), 32)
@@ -663,18 +670,26 @@
     early = tuple(t for t in range(len(STREAMS)) if t not in late)
 
     def results(layer):
-        return (g_ref.at[layer], gsmall_ref.at[layer], ghidden_ref.at[layer], gbias_ref.at[layer])
+        return (g_ref.at[layer], gsmall_ref.at[layer], ghidden_ref.at[layer], gbias_ref.at[pl.ds(layer * 16, 16)])
 
     scratch = (low_ref, turned_ref, du_ref, dqkv_ref, do_ref)
 
+    def after_mlp1():
+        send_core(1, (1,))
+        send_core(1, (0,), begin=UP0)
+
+    def after_proj1():
+        send_core(1, (0,), end=UP0)
+        add_core(1, (1,))
+        send(1, (1,), 0)
+
     def before_attend1():
-        for t in (1, 0):
-            add_core(1, (t,))
-            send(1, (t,), 0)
+        add_core(1, (0,))
+        send(1, (0,), 0)
 
     dx1 = backward_body(
         params(1), saved(1), x_ref.at[1], dy_ref, results(1), scratch,
-        after_mlp=lambda: send_core(1, (1,)), after_proj=lambda: send_core(1, (0,)),
+        after_mlp=after_mlp1, after_proj=after_proj1,
         before_attend=before_attend1, after_weights=lambda: send_core(1, late),
     )
     in_token_order(1, dx1, dx_ref.at[1], dy_ref)
@@ -689,17 +704,21 @@
     def after_mlp0():
         pl.semaphore_wait(free_sem, 1)
         send_core(0, (1,))
+        send_core(0, (0,), begin=UP0)
+
+    def after_proj0():
+        send_core(0, (0,), end=UP0)
+        add_core(0, (1,))
+        send(0, (1,), 0)
+
+    def before_attend0():
+        add_core(0, (0,))
+        send(0, (0,), 0)
+
+    def after_attend0():
+        add(1, early, 1)
         add(1, late, 0)
         send(1, late, 1)
-
-    def before_attend0():
-        for t in (1, 0):
-            add_core(0, (t,))
-            send(0, (t,), 0)
-
-    def after_attend0():
-        add(1, early, 1)
-        add(1, late, 1)
 
     def after_weights0():
         send_core(0, late)
@@ -708,7 +727,7 @@
 
     dx0 = backward_body(
         params(0), saved(0), x_ref.at[0], dy_ref, results(0), scratch,
-        in_mlp=in_mlp0, after_mlp=after_mlp0, after_proj=lambda: send_core(0, (0,)),
+        in_mlp=in_mlp0, after_mlp=after_mlp0, after_proj=after_proj0,
         before_attend=before_attend0, after_attend=after_attend0, after_weights=after_weights0,
     )
     add_core(0, late)
@@ -720,8 +739,10 @@
     add(0, (0,), 0)
     send(0, (0,), 1)
 
+    add(0, (1,), 1)
+    send_y((1,))
+    gtable = table_sums(gbias_ref, places_ref)
     for layer in range(2):
-        gtable = table_sums(gbias_ref.at[layer], places_ref)
         for shard in range(4):
             half, core = shard // 2, shard % 2
             y = half * 2 + layer
@@ -730,12 +751,15 @@
             for j in range(4):
                 at = shard * 512 + j * 128
                 sums_in[core, y, 8 + j : 9 + j, 0:128] = ghidden_ref[layer, :, at : at + 128]
-            sums_in[core, y, 16:20] = gtable[shard * 4 : shard * 4 + 4]
+            sums_in[core, y, 16:20] = gtable[layer * 16 + shard * 4 : layer * 16 + shard * 4 + 4]
     small_copy = copies.start(sums_in.at[1 - me["core"]], sums_core, partner)
-    add(0, early, 1)
-    send_y(early)
     add(0, late, 0)
     send(0, late, 1)
+    add(0, (0,), 1)
+    send_y((0,))
+    add(1, late, 1)
+    add_y((1,))
+    spread((1,), 0)
     small_copy.wait_recv()
     sums_own[0] = sums_in[me["core"]] + sums_core[...]
     small_sent = [
@@ -749,8 +773,8 @@
         start = sums_own[0, me["y"]] if stage == 0 else sums_own[stage, 0]
         return start + sums_land[stage, 0] + sums_land[stage, 1] + sums_land[stage, 2]
 
-    add_y(early)
-    spread(early, 0)
+    add_y((0,))
+    spread((0,), 0)
     add(0, late, 1)
     send_y(late)
     for stage, axis in enumerate("xz", 1):
@@ -820,7 +844,7 @@
             tuple(pltpu.VMEM((3, 32, (hi - lo) // 4), BF16) for lo, hi, _ in STREAMS),
             pltpu.VMEM((128, PACKED), BF16),
             pltpu.VMEM((32, PAIR, KEYS), F32),
-            pltpu.VMEM((2, 16, PAIR, KEYS), F32),
+            pltpu.VMEM((32, PAIR, KEYS), F32),
             low,
             pltpu.VMEM((D, ROWS), BF16),
             pltpu.VMEM((ROWS, D), F32),
@@ -914,7 +938,7 @@
     slots = jnp.arange(2 * IMGS, dtype=jnp.int32)
     inverse = jnp.sum(jnp.where(slot_order[:, None] == slots[None, :], slots[:, None], 0), axis=0)
     picks = jnp.where(first_section, inverse, slots)
-    input_grad = jnp.take(dx_slots[:, :TOK], picks, axis=0).astype(F32)
+    input_grad = jnp.take(dx_slots[:, :TOK], picks, axis=0, mode="clip").astype(F32)
     down = jnp.concatenate(
         [share[:, DOWN0 + k * D : DOWN0 + (k + 1) * D] for k in range(4)], axis=0
     )

time: 174 us -> 173 us (level)
  no operation moved by 1% of the time
where the time goes in v4:
time: 173 us
  Pallas kernels  152 us (88%)
  local copies, waits for them, and re-layouts  14.7 us (8%)
  other arithmetic  5.65 us (3%)
    pallas_call x1, Pallas kernels, train(): pl.pallas_call(train_kernel, out_shape=[jax.ShapeDtypeStruct(tokens, BF16...  152 us
    unnamed x29, local copies, waits for them, and re-layouts  7.4 us

profile of v4, /device:TPU:0, one launch (start us, length us, event | category | flops | bytes accessed | tf_op | source)
XLA Modules:
  0.0 172.8 jit_solution(4357291684301418458)
XLA Ops:
  0.7 0.0 copy-start.5
  0.7 0.0 copy-start.3
  0.7 2.2 %copy.40.images_ref = bf16[4,196,512]{2,1,0:T(8,128)(2,1)} copy(bf16[4,196,512]{2,0,1:T(4,128)(2,1)} %param.18) | data formatting | bytes 1605632 | tf_op args[0]
  3.0 1.0 copy.41.cot_hbm
  4.0 0.0 copy-done.8
  4.1 0.6 fusion.5.tiny_ref
  4.7 0.0 copy-done.4
  4.7 0.6 pad.30.places_ref
  5.3 0.1 reshape.128
  5.4 0.1 reshape.129
  5.5 0.1 eq.38
  5.6 0.1 select_select_fusion
  5.7 0.7 pad_maximum_fusion.mask_ref
  6.5 151.6 %train_layers.1 = (bf16[4,208,512]{2,1,0:T(8,128)(2,1)}, bf16[4,208,512]{2,1,0:T(8,128)(2,1)}, bf16[128,6144]{1,0:T(8,128)(2,1)}, f32[24,256]{1,0:T(8,128)}) custom-call(s32[4]{0:T(128)} %bitcast.49, bf16[4,196,512]{2,1,0:T(8,128)(2,1)} %copy.40.images_ref, bf16[4,196,512]{2,1,0:T(8,128)(2,1)} %copy.41.cot_hbm, bf16[1,128,1536]{2,1,0:T(8,128)(2,1)} %qkv_hbm.1, ...), custom_call_target="tpu_custom_call" | custom-call | flops 16911433728 | bytes 16777216 | tf_op jit(solution)/shard_map/train_layers/pallas_call | solution.py:825
  158.1 1.3 slice_bitcast_fusion
  159.4 0.0 copy-start.11
  159.4 1.3 copy.42
  160.7 0.1 slice.40
  160.8 0.0 copy-done.11
  160.8 0.1 select_reduce_fusion
  160.9 0.6 gather_fusion
  161.5 0.2 bitcast_convert_fusion
  161.7 2.2 %copy.43 = f32[1,4,196,512]{3,1,2,0:T(4,128)} copy(f32[1,4,196,512]{3,2,1,0:T(8,128)S(1)} %bitcast_convert_fusion) | data formatting | bytes 3211264
  163.9 1.0 bitcast_convert_fusion.2
  164.8 0.8 slice_bitcast_fusion.4
  165.6 1.1 bitcast_convert_fusion.1
  166.7 1.1 maximum_convert_fusion
  167.8 1.3 slice_bitcast_fusion.6
  169.1 1.2 slice_bitcast_fusion.7
  170.3 0.7 slice_bitcast_fusion.5
  171.0 0.6 copy.44
  171.6 1.3 slice.51
  (25 shorter events, 0.1 us)
Async XLA Ops:
  0.6 2.3 %copy-start.1 = (bf16[4,196,512]{2,0,1:T(4,128)(2,1)S(1)}, bf16[4,196,512]{2,0,1:T(4,128)(2,1)}, u32[]{:S(2)}) copy-start(bf16[4,196,512]{2,0,1:T(4,128)(2,1)} %param.19) | copy-start | bytes 2408452
  0.7 3.4 %copy-start.7 = (bf16[1,512]{1,0:T(2,128)(2,1)S(1)}, bf16[1,512]{1,0:T(2,128)(2,1)}, u32[]{:S(2)}) copy-start(bf16[1,512]{1,0:T(2,128)(2,1)} %param.30) | copy-start | bytes 3076
  0.7 3.4 %copy-start.8 = (bf16[1,6,128]{2,1,0:T(8,128)(2,1)S(1)}, bf16[1,6,128]{2,1,0:T(8,128)(2,1)}, u32[]{:S(2)}) copy-start(bf16[1,6,128]{2,1,0:T(8,128)(2,1)} %param.29) | copy-start | bytes 4612
  0.7 3.4 %copy-start.10 = (bf16[1,2,128]{2,1,0:T(2,128)(2,1)S(1)}, bf16[1,2,128]{2,1,0:T(2,128)(2,1)}, u32[]{:S(2)}) copy-start(bf16[1,2,128]{2,1,0:T(2,128)(2,1)} %param.28) | copy-start | bytes 1540
  0.7 3.4 %copy-start.6 = (bf16[1,169,4]{1,2,0:T(4,128)(2,1)S(1)}, bf16[1,169,4]{1,2,0:T(4,128)(2,1)}, u32[]{:S(2)}) copy-start(bf16[1,169,4]{1,2,0:T(4,128)(2,1)} %param.27) | copy-start | bytes 4060
  0.7 4.0 %copy-start.4 = (s32[49,49]{1,0:T(8,128)S(1)}, s32[49,49]{1,0:T(8,128)}, u32[]{:S(2)}) copy-start(s32[49,49]{1,0:T(8,128)} %param.22) | copy-start | bytes 28816
  0.7 4.6 %copy-start.9 = (s32[196]{0:T(256)S(1)}, s32[196]{0:T(256)}, u32[]{:S(2)}) copy-start(s32[196]{0:T(256)} %param.21) | copy-start | bytes 2356
  0.7 4.9 %copy-start.5 = (pred[112,128]{1,0:T(8,128)(4,1)S(1)}, pred[112,128]{1,0:T(8,128)(4,1)}, u32[]{:S(2)}) copy-start(pred[112,128]{1,0:T(8,128)(4,1)} %constant.58) | copy-start | bytes 43012
  0.7 5.0 %copy-start.3 = (f32[1,2,112,128]{3,2,1,0:T(8,128)S(1)}, f32[1,2,112,128]{3,2,1,0:T(8,128)}, u32[]{:S(2)}) copy-start(f32[1,2,112,128]{3,2,1,0:T(8,128)} %constant.57) | copy-start | bytes 344068
  158.1 2.6 %copy-start.2 = (bf16[4,208,512]{2,1,0:T(8,128)(2,1)S(1)}, bf16[4,208,512]{2,1,0:T(8,128)(2,1)}, u32[]{:S(2)}) copy-start(bf16[4,208,512]{2,1,0:T(8,128)(2,1)} %get-tuple-element.15) | copy-start | bytes 2555908
  159.4 1.4 copy-start.11
  161.7 2.2 %copy-start = (bf16[128,6144]{1,0:T(8,128)(2,1)S(1)}, bf16[128,6144]{1,0:T(8,128)(2,1)}, u32[]{:S(2)}) copy-start(bf16[128,6144]{1,0:T(8,128)(2,1)} %get-tuple-element.16) | copy-start | bytes 4718596

commit v5 on v4

--- a/solution.py
+++ b/solution.py
@@ -730,14 +730,14 @@
         in_mlp=in_mlp0, after_mlp=after_mlp0, after_proj=after_proj0,
         before_attend=before_attend0, after_attend=after_attend0, after_weights=after_weights0,
     )
+    add(0, (0,), 0)
+    send(0, (0,), 1)
     add_core(0, late)
     send(0, late, 0)
     in_token_order(0, dx0, dx_ref.at[0], None)
     dx_copy = copies.start(dx_ref.at[1 - pipe], dx_land, neighbour)
     dx_keep = pltpu.make_async_copy(dx_ref.at[pipe], dx_hbm.at[pl.ds(pipe * IMGS, IMGS)], local_sem.at[1])
     dx_keep.start()
-    add(0, (0,), 0)
-    send(0, (0,), 1)
 
     add(0, (1,), 1)
     send_y((1,))

time: 173 us -> 176 us (1.017)
  Pallas kernels: 152 us -> 155 us
    pallas_call x1, Pallas kernels: 152 us -> 155 us  [train(): pl.pallas_call(train_kernel, out_shape=[jax.ShapeDtypeStruct(tokens, BF16...]
where the time goes in v5:
time: 176 us
  Pallas kernels  155 us (88%)
  local copies, waits for them, and re-layouts  14.7 us (8%)
  other arithmetic  5.65 us (3%)
    pallas_call x1, Pallas kernels, train(): pl.pallas_call(train_kernel, out_shape=[jax.ShapeDtypeStruct(tokens, BF16...  155 us
    unnamed x29, local copies, waits for them, and re-layouts  7.4 us

profile of v5, /device:TPU:0, one launch (start us, length us, event | category | flops | bytes accessed | tf_op | source)
XLA Modules:
  0.0 175.9 jit_solution(3949873746431127766)
XLA Ops:
  0.7 0.0 copy-start.5
  0.7 0.0 copy-start.3
  0.7 2.2 %copy.40.images_ref = bf16[4,196,512]{2,1,0:T(8,128)(2,1)} copy(bf16[4,196,512]{2,0,1:T(4,128)(2,1)} %param.18) | data formatting | bytes 1605632 | tf_op args[0]
  3.0 1.0 copy.41.cot_hbm
  4.1 0.6 fusion.5.tiny_ref
  4.7 0.6 pad.30.places_ref
  5.3 0.0 copy-done.9
  5.3 0.1 reshape.128
  5.4 0.1 reshape.129
  5.5 0.1 eq.38
  5.6 0.1 select_select_fusion
  5.7 0.7 pad_maximum_fusion.mask_ref
  6.5 154.7 %train_layers.1 = (bf16[4,208,512]{2,1,0:T(8,128)(2,1)}, bf16[4,208,512]{2,1,0:T(8,128)(2,1)}, bf16[128,6144]{1,0:T(8,128)(2,1)}, f32[24,256]{1,0:T(8,128)}) custom-call(s32[4]{0:T(128)} %bitcast.49, bf16[4,196,512]{2,1,0:T(8,128)(2,1)} %copy.40.images_ref, bf16[4,196,512]{2,1,0:T(8,128)(2,1)} %copy.41.cot_hbm, bf16[1,128,1536]{2,1,0:T(8,128)(2,1)} %qkv_hbm.1, ...), custom_call_target="tpu_custom_call" | custom-call | flops 16911433728 | bytes 16777216 | tf_op jit(solution)/shard_map/train_layers/pallas_call | solution.py:825
  161.2 0.0 copy-start.2
  161.2 1.3 slice_bitcast_fusion
  162.5 0.0 copy-start.11
  162.5 1.3 copy.42
  163.8 0.1 slice.40
  163.9 0.1 select_reduce_fusion
  164.0 0.6 gather_fusion
  164.6 0.2 bitcast_convert_fusion
  164.8 2.2 %copy.43 = f32[1,4,196,512]{3,1,2,0:T(4,128)} copy(f32[1,4,196,512]{3,2,1,0:T(8,128)S(1)} %bitcast_convert_fusion) | data formatting | bytes 3211264
  167.0 0.0 copy-done
  167.0 1.0 bitcast_convert_fusion.2
  167.9 0.8 slice_bitcast_fusion.4
  168.7 1.1 bitcast_convert_fusion.1
  169.8 1.1 maximum_convert_fusion
  170.9 1.3 slice_bitcast_fusion.6
  172.2 1.2 slice_bitcast_fusion.7
  173.4 0.7 slice_bitcast_fusion.5
  174.1 0.6 copy.44
  174.7 1.3 slice.51
  (25 shorter events, 0.1 us)
Async XLA Ops:
  0.6 2.3 %copy-start.1 = (bf16[4,196,512]{2,0,1:T(4,128)(2,1)S(1)}, bf16[4,196,512]{2,0,1:T(4,128)(2,1)}, u32[]{:S(2)}) copy-start(bf16[4,196,512]{2,0,1:T(4,128)(2,1)} %param.19) | copy-start | bytes 2408452
  0.7 3.4 %copy-start.7 = (bf16[1,512]{1,0:T(2,128)(2,1)S(1)}, bf16[1,512]{1,0:T(2,128)(2,1)}, u32[]{:S(2)}) copy-start(bf16[1,512]{1,0:T(2,128)(2,1)} %param.30) | copy-start | bytes 3076
  0.7 3.4 %copy-start.8 = (bf16[1,6,128]{2,1,0:T(8,128)(2,1)S(1)}, bf16[1,6,128]{2,1,0:T(8,128)(2,1)}, u32[]{:S(2)}) copy-start(bf16[1,6,128]{2,1,0:T(8,128)(2,1)} %param.29) | copy-start | bytes 4612
  0.7 3.4 %copy-start.10 = (bf16[1,2,128]{2,1,0:T(2,128)(2,1)S(1)}, bf16[1,2,128]{2,1,0:T(2,128)(2,1)}, u32[]{:S(2)}) copy-start(bf16[1,2,128]{2,1,0:T(2,128)(2,1)} %param.28) | copy-start | bytes 1540
  0.7 3.4 %copy-start.6 = (bf16[1,169,4]{1,2,0:T(4,128)(2,1)S(1)}, bf16[1,169,4]{1,2,0:T(4,128)(2,1)}, u32[]{:S(2)}) copy-start(bf16[1,169,4]{1,2,0:T(4,128)(2,1)} %param.27) | copy-start | bytes 4060
  0.7 4.0 %copy-start.4 = (s32[49,49]{1,0:T(8,128)S(1)}, s32[49,49]{1,0:T(8,128)}, u32[]{:S(2)}) copy-start(s32[49,49]{1,0:T(8,128)} %param.22) | copy-start | bytes 28816
  0.7 4.6 %copy-start.9 = (s32[196]{0:T(256)S(1)}, s32[196]{0:T(256)}, u32[]{:S(2)}) copy-start(s32[196]{0:T(256)} %param.21) | copy-start | bytes 2356
  0.7 4.9 %copy-start.5 = (pred[112,128]{1,0:T(8,128)(4,1)S(1)}, pred[112,128]{1,0:T(8,128)(4,1)}, u32[]{:S(2)}) copy-start(pred[112,128]{1,0:T(8,128)(4,1)} %constant.58) | copy-start | bytes 43012
  0.7 5.0 %copy-start.3 = (f32[1,2,112,128]{3,2,1,0:T(8,128)S(1)}, f32[1,2,112,128]{3,2,1,0:T(8,128)}, u32[]{:S(2)}) copy-start(f32[1,2,112,128]{3,2,1,0:T(8,128)} %constant.57) | copy-start | bytes 344068
  161.2 2.6 %copy-start.2 = (bf16[4,208,512]{2,1,0:T(8,128)(2,1)S(1)}, bf16[4,208,512]{2,1,0:T(8,128)(2,1)}, u32[]{:S(2)}) copy-start(bf16[4,208,512]{2,1,0:T(8,128)(2,1)} %get-tuple-element.15) | copy-start | bytes 2555908
  162.5 1.4 copy-start.11
  164.8 2.2 %copy-start = (bf16[128,6144]{1,0:T(8,128)(2,1)S(1)}, bf16[128,6144]{1,0:T(8,128)(2,1)}, u32[]{:S(2)}) copy-start(bf16[128,6144]{1,0:T(8,128)(2,1)} %get-tuple-element.16) | copy-start | bytes 4718596
